TPU v7x, 1024 devices: a whole 8x8x8 slice. The times are simulated.
1024 devices in a mesh: dp: 8 (over z), pipe: 16 (over y, core), expert: 8 (over x).
Axes of the slice: x: 8, y: 8, z: 8, core: 2. Of those that a mesh axis runs over, the one named last changes fastest.
Arguments:
- tokens: bfloat16 [6144, 3072], P(('dp', 'expert')), may hold values from -6 to 6
- routes: int32 [6144, 2], P(('dp', 'expert')), may hold values from 0 to 7, all different within a row; in each aligned block of 96 rows (0 to 95, 96 to 191, ...) at most 32 rows name the same one
- route_weights: float32 [6144, 2], P(('dp', 'expert')), may hold values from 0.2 to 1
- w_gate: bfloat16 [8, 3072, 8192], P('expert', None, 'pipe'), may hold values from -0.109375 to 0.109375
- w_up: bfloat16 [8, 3072, 8192], P('expert', None, 'pipe'), may hold values from -0.109375 to 0.109375
- w_down: bfloat16 [8, 8192, 3072], P('expert', 'pipe'), may hold values from -0.0625 to 0.0625
Outputs:
- mixed: bfloat16 [6144, 3072], P(('dp', 'expert'), 'pipe')
Inputs may be any that keep to these rules, and one draw needn't show every extreme that they name: `routes`: each row names two different experts. Among the 96 rows of one block no expert is named more than 32 times, a bound that some block reaches.
All inputs are finite; a program needn't handle non-finite values.
Results may differ from a plain program's by a relative error of at most 0.019.
Values may be sent and summed in bfloat16 or wider, within the bound.
A program may use at most 64 MiB of HBM per device.

v0:
```python
import jax
import jax.numpy as jnp
from jax import lax
from jax.sharding import PartitionSpec as P


def cut_along(x, dim, peers):
    before, after = (x.shape[:dim], x.shape[dim + 1 :])
    return jnp.moveaxis(x.reshape(*before, peers, -1, *after), dim, 0)


def sum_at_owner(x, axis, dim):
    peers = lax.axis_size(axis)
    pieces = lax.all_to_all(cut_along(x, dim, peers), axis, 0, 0, tiled=True)
    return jnp.sum(pieces.astype(jnp.float32), axis=0)


def slot_table(route_rows, expert_total):
    choices = route_rows.reshape(-1)
    expert_ids = jnp.arange(expert_total, dtype=jnp.int32)
    matches = (choices[None, :] == expert_ids[:, None]).astype(jnp.int32)
    rank_of = jnp.cumsum(matches, axis=1) - 1
    return (choices, jnp.sum(rank_of * matches, axis=0))


def on_device(tokens, routes, route_weights, w_gate, w_up, w_down):
    expert_count = lax.axis_size("expert")
    pipe_count = lax.axis_size("pipe")
    replica_count = lax.axis_size("dp")
    expert_total = w_gate.shape[0] * expert_count
    hidden_width = w_gate.shape[2]
    tok_rows = tokens.shape[0]
    model_width = tokens.shape[1]
    capacity = min(
        tok_rows,
        replica_count * ((2 * tok_rows + expert_total - 1) // expert_total // replica_count + 1),
    )
    slot_share = capacity // replica_count
    col_share = model_width // pipe_count
    group_count = replica_count * expert_total
    choices, slot_of = slot_table(routes, expert_total)
    target = (
        slot_of // slot_share * (expert_total * slot_share)
        + choices * slot_share
        + slot_of % slot_share
    )
    column_ids = jnp.arange(group_count * slot_share, dtype=jnp.int32)
    picker = (column_ids[:, None] == target[None, :]).astype(jnp.bfloat16)
    gate_full = w_gate[0]
    up_full = w_up[0]
    doubled = jnp.repeat(tokens, 2, axis=0)
    outgoing = jnp.dot(picker, doubled, preferred_element_type=jnp.float32)
    outgoing = outgoing.astype(jnp.bfloat16).reshape(group_count, slot_share, model_width)
    arrived = lax.all_to_all(outgoing, ("dp", "expert"), split_axis=0, concat_axis=0, tiled=True)
    gate_values = jnp.einsum("gsd,df->gsf", arrived, gate_full, preferred_element_type=jnp.float32)
    up_values = jnp.einsum("gsd,df->gsf", arrived, up_full, preferred_element_type=jnp.float32)
    hidden = (jax.nn.silu(gate_values) * up_values).astype(jnp.bfloat16)
    down_blocks = w_down[0].reshape(hidden_width, pipe_count, col_share)
    block_term = jnp.einsum(
        "gsf,fke->kgse", hidden, down_blocks, preferred_element_type=jnp.float32
    )
    block_term = lax.optimization_barrier(block_term.astype(jnp.bfloat16))
    section = sum_at_owner(block_term.astype(jnp.float32).astype(jnp.bfloat16), "pipe", 0)
    summed = section.astype(jnp.bfloat16).reshape(group_count, slot_share, col_share)
    returned = lax.all_to_all(summed, ("dp", "expert"), split_axis=0, concat_axis=0, tiled=True)
    mixing = (target[:, None] == column_ids[None, :]).astype(jnp.float32) * route_weights.reshape(
        -1
    )[:, None]
    mixing = mixing.reshape(tok_rows, 2, group_count * slot_share).sum(axis=1)
    mixed_out = jnp.dot(
        mixing, returned.reshape(group_count * slot_share, col_share).astype(jnp.float32)
    )
    return mixed_out.astype(jnp.bfloat16)


def solution(mesh):
    return jax.shard_map(
        on_device,
        mesh=mesh,
        in_specs=(
            P(("dp", "expert"), None),
            P(("dp", "expert"), None),
            P(("dp", "expert"), None),
            P("expert", None, "pipe"),
            P("expert", None, "pipe"),
            P("expert", "pipe", None),
        ),
        out_specs=P(("dp", "expert"), "pipe"),
        check_vma=False,
    )
```

profile of v0, /device:TPU:1, one launch (start us, length us, event | category | flops | bytes accessed | tf_op | source)
XLA Modules:
  0.0 173.3 jit_solution(2709984627360493047)
XLA Ops:
  0.0 0.0 copy-start
  0.0 0.9 copy.57
  0.9 0.1 eq.44
  1.1 0.6 reduce-window.6
  1.7 0.2 slice_reduce_fusion
  1.9 0.1 add_bitcast_fusion
  2.1 2.7 %broadcast_in_dim.2 = bf16[96,2,3072]{2,1,0:T(2,128)(2,1)} broadcast(bf16[96,3072]{1,0:T(8,128)(2,1)} %param.6), dimensions={0,2} | broadcast | bytes 1769472 | tf_op jit(solution)/shard_map/broadcast_in_dim | solution.py:51
  4.7 3.7 %reshape.117 = bf16[192,3072]{1,0:T(8,128)(2,1)} reshape(bf16[96,2,3072]{2,1,0:T(2,128)(2,1)} %broadcast_in_dim.2) | data formatting | bytes 2359296 | tf_op jit(solution)/shard_map/reshape | solution.py:51
  8.4 3.0 %convolution_convert_fusion = bf16[256,3072]{1,0:T(8,128)(2,1)} fusion(bf16[192,3072]{1,0:T(8,128)(2,1)} %reshape.117, s32[192]{0:T(256)S(1)} %fusion.35), kind=kOutput, calls=%fused_computation | convolution fusion | flops 302825472 | bytes 2753280 | tf_op jit(solution)/shard_map/dot_general | solution.py:52
  11.4 3.9 %reshape.118 = bf16[64,4,3072]{2,1,0:T(4,128)(2,1)} reshape(bf16[256,3072]{1,0:T(8,128)(2,1)} %convolution_convert_fusion) | data formatting | bytes 3145728 | tf_op jit(solution)/shard_map/reshape | solution.py:53
  15.3 23.4 %all-to-all-start = ((bf16[64,4,3072]{2,1,0:T(4,128)(2,1)}), bf16[64,4,3072]{2,1,0:T(4,128)(2,1)}, u32[]{:S(2)}, u32[]{:S(2)}) async-start(bf16[64,4,3072]{2,1,0:T(4,128)(2,1)} %reshape.118), calls=%async_computation | async-start | bytes 3145728 | tf_op jit(solution)/shard_map/all_to_all | solution.py:54
  38.7 4.7 %copy.64 = bf16[1,512,3072]{1,2,0:T(8,128)(2,1)} copy(bf16[1,512,3072]{2,1,0:T(8,128)(2,1)} %param.11) | data formatting | bytes 6291456 | tf_op args[5]
  43.3 34.2 %all-to-all-done = bf16[64,4,3072]{2,1,0:T(4,128)(2,1)} async-done(((bf16[64,4,3072]{2,1,0:T(4,128)(2,1)}), bf16[64,4,3072]{2,1,0:T(4,128)(2,1)}, u32[]{:S(2)}, u32[]{:S(2)}) %all-to-all-start) | async-done | bytes 1572896 | tf_op jit(solution)/shard_map/all_to_all | solution.py:54
  77.5 4.2 %fusion.2 = f32[64,4,512]{2,0,1:T(8,128)} fusion(bf16[1,3072,512]{2,1,0:T(8,128)(2,1)} %param.9, bf16[64,4,3072]{2,1,0:T(4,128)(2,1)} %all-to-all-done), kind=kOutput, calls=%fused_computation.3 | convolution fusion | flops 805306368 | bytes 5242880 | tf_op jit(solution)/shard_map/gsd,df->gsf/dot_general | solution.py:55
  81.7 0.0 copy-done
  81.7 6.1 %convert_bitcast_fusion = bf16[16,64,4,192]{3,1,0,2:T(8,128)(2,1)} fusion(bf16[512,16,192,1]{0,2,1,3:T(8,128)(2,1)} %bitcast.36, bf16[1,3072,512]{2,1,0:T(8,128)(2,1)S(1)} %copy-done, bf16[64,4,3072]{2,1,0:T(4,128)(2,1)} %all-to-all-done, f32[64,4,512]{2,0,1:T(8,128)} %fusion.2), kind=kOutput, calls=%fused_computation.5 | convolution fusion | flops 1612185600 | bytes 9961472 | tf_op jit(solution)/shard_map/gsf,fke->kgse/dot_general | solution.py:59
  87.8 3.2 %copy.65 = bf16[16,1,64,4,192]{4,2,3,1,0:T(8,128)(2,1)} copy(bf16[16,1,64,4,192]{4,2,0,3,1:T(8,128)(2,1)} %bitcast.37) | data formatting | bytes 3145728 | tf_op jit(solution)/shard_map/reshape | solution.py:9
  91.0 10.8 %all-to-all-start.1 = ((bf16[16,1,64,4,192]{4,2,3,1,0:T(8,128)(2,1)}), bf16[16,1,64,4,192]{4,2,3,1,0:T(8,128)(2,1)}, u32[]{:S(2)}, u32[]{:S(2)}) async-start(bf16[16,1,64,4,192]{4,2,3,1,0:T(8,128)(2,1)} %copy.65), calls=%async_computation.1 | async-start | bytes 4194304 | tf_op jit(solution)/shard_map/all_to_all | solution.py:14
  101.8 0.0 copy-start.1
  101.8 0.0 copy-start.2
  101.8 0.1 reduce_sum.33
  101.9 0.1 copy.58
  102.0 48.8 %all-to-all-done.1 = bf16[16,1,64,4,192]{4,2,3,1,0:T(8,128)(2,1)} async-done(((bf16[16,1,64,4,192]{4,2,3,1,0:T(8,128)(2,1)}), bf16[16,1,64,4,192]{4,2,3,1,0:T(8,128)(2,1)}, u32[]{:S(2)}, u32[]{:S(2)}) %all-to-all-start.1) | async-done | bytes 1572896 | tf_op jit(solution)/shard_map/all_to_all | solution.py:14
  150.8 2.0 %reduce_sum.35 = bf16[64,4,192]{2,0,1:T(8,128)(2,1)S(1)} reduce(bf16[16,1,64,4,192]{4,2,3,1,0:T(8,128)(2,1)} %all-to-all-done.1, bf16[]{:T(256)} %constant.49.clone.1), dimensions={0,1}, to_apply=%region_4.5 | reduce | flops 737280 | bytes 1671170 | tf_op jit(solution)/shard_map/reduce_sum | solution.py:15
  152.8 0.7 copy.67
  153.6 7.3 %all-to-all-start.2 = ((bf16[64,4,192]{2,1,0:T(4,128)(2,1)}), bf16[64,4,192]{2,1,0:T(4,128)(2,1)S(1)}, u32[]{:S(2)}, u32[]{:S(2)}) async-start(bf16[64,4,192]{2,1,0:T(4,128)(2,1)} %copy.67), calls=%async_computation.2 | async-start | bytes 262144 | tf_op jit(solution)/shard_map/all_to_all | solution.py:65
  160.9 0.0 copy-done.1
  160.9 0.0 copy-done.2
  160.9 0.1 select_reduce_fusion
  161.1 11.4 %all-to-all-done.2 = bf16[64,4,192]{2,1,0:T(4,128)(2,1)S(1)} async-done(((bf16[64,4,192]{2,1,0:T(4,128)(2,1)}), bf16[64,4,192]{2,1,0:T(4,128)(2,1)S(1)}, u32[]{:S(2)}, u32[]{:S(2)}) %all-to-all-start.2) | async-done | bytes 98336 | tf_op jit(solution)/shard_map/all_to_all | solution.py:65
  172.5 0.1 reshape.120
  172.5 0.8 fusion.37
  (7 shorter events, 0.1 us)
Async XLA Ops:
  0.0 81.7 %copy-start = (bf16[1,3072,512]{2,1,0:T(8,128)(2,1)S(1)}, bf16[1,3072,512]{2,1,0:T(8,128)(2,1)}, u32[]{:S(2)}) copy-start(bf16[1,3072,512]{2,1,0:T(8,128)(2,1)} %param.10) | copy-start | bytes 9437188
  15.3 62.3 %all-to-all-start = ((bf16[64,4,3072]{2,1,0:T(4,128)(2,1)}), bf16[64,4,3072]{2,1,0:T(4,128)(2,1)}, u32[]{:S(2)}, u32[]{:S(2)}) async-start(bf16[64,4,3072]{2,1,0:T(4,128)(2,1)} %reshape.118), calls=%async_computation | async-start | bytes 3145728 | tf_op jit(solution)/shard_map/all_to_all | solution.py:54
  91.0 59.9 %all-to-all-start.1 = ((bf16[16,1,64,4,192]{4,2,3,1,0:T(8,128)(2,1)}), bf16[16,1,64,4,192]{4,2,3,1,0:T(8,128)(2,1)}, u32[]{:S(2)}, u32[]{:S(2)}) async-start(bf16[16,1,64,4,192]{4,2,3,1,0:T(8,128)(2,1)} %copy.65), calls=%async_computation.1 | async-start | bytes 4194304 | tf_op jit(solution)/shard_map/all_to_all | solution.py:14
  101.8 59.1 %copy-start.1 = (s32[96,2]{0,1:T(2,128)S(1)}, s32[96,2]{0,1:T(2,128)}, u32[]{:S(2)}) copy-start(s32[96,2]{0,1:T(2,128)} %param.7) | copy-start | bytes 2308
  101.8 59.1 %copy-start.2 = (f32[96,2]{0,1:T(2,128)S(1)}, f32[96,2]{0,1:T(2,128)}, u32[]{:S(2)}) copy-start(f32[96,2]{0,1:T(2,128)} %param.8) | copy-start | bytes 2308
  153.6 18.9 %all-to-all-start.2 = ((bf16[64,4,192]{2,1,0:T(4,128)(2,1)}), bf16[64,4,192]{2,1,0:T(4,128)(2,1)S(1)}, u32[]{:S(2)}, u32[]{:S(2)}) async-start(bf16[64,4,192]{2,1,0:T(4,128)(2,1)} %copy.67), calls=%async_computation.2 | async-start | bytes 262144 | tf_op jit(solution)/shard_map/all_to_all | solution.py:65
where the time goes:
time: 174 us; the launch traced here: 173 us
  waiting for transfers between devices  94.4 us (54%)
  starting transfers between devices  41.5 us (24%)
  local copies, waits for them, and re-layouts  20.4 us (12%)
  matrix products  14 us (8%)
  other arithmetic  2.88 us (2%)
    all_to_all x1, waiting for transfers between devices, sum_at_owner(): pieces = lax.all_to_all(cut_along(x, dim, peers), axis, 0, 0, tiled=True)  48.8 us
    all_to_all x1, waiting for transfers between devices, on_device(): lax.all_to_all(outgoing, ('dp', 'expert'), split_axis=0, concat_axis=0, t...  34.2 us
    all_to_all x1, starting transfers between devices, on_device(): lax.all_to_all(outgoing, ('dp', 'expert'), split_axis=0, concat_axis=0, t...  23.4 us
    all_to_all x1, waiting for transfers between devices, on_device(): lax.all_to_all(summed, ('dp', 'expert'), split_axis=0, concat_axis=0, til...  11.4 us
    all_to_all x1, starting transfers between devices, sum_at_owner(): pieces = lax.all_to_all(cut_along(x, dim, peers), axis, 0, 0, tiled=True)  10.8 us
    all_to_all x1, starting transfers between devices, on_device(): lax.all_to_all(summed, ('dp', 'expert'), split_axis=0, concat_axis=0, til...  7.32 us
    dot_general x1, matrix products, on_device(): jnp.einsum('gsf,fke->kgse', hidden, down_blocks, preferred_element_type=j...  6.08 us
    unnamed x8, local copies, waits for them, and re-layouts  5.6 us
  transfers between devices with their start and end apart: 3, of which 3 were waited for; matrix products, arithmetic and copies ran while one was open for 3% of the time, Pallas kernels for 0%

commit v1 on v0

v1 whole, which is shorter than its diff:
```python
import functools

import jax
import jax.numpy as jnp
from jax import lax
from jax.experimental import pallas as pl
from jax.experimental.pallas import tpu as pltpu
from jax.sharding import PartitionSpec as P

MESH = pl.DeviceIdType.MESH
F32 = jnp.float32
BF16 = jnp.bfloat16


def kernel(
    dims,
    tokens,
    routes,
    route_w,
    wg,
    wu,
    wd,
    out,
    tok_v,
    xs,
    xbuf,
    wg_v,
    wu_v,
    wd_v,
    acc_g,
    acc_u,
    hid,
    mix,
    pk,
    cin,
    rin,
    rout,
    fin,
    rbuf,
    load_sem,
    xs_sem,
    xr_sem,
    os_sem,
    or_sem,
    ys_sem,
    yr_sem,
    cs_sem,
    cr_sem,
    ds_sem,
    dr_sem,
    rs_sem,
    rr_sem,
    fs_sem,
    fr_sem,
):
    ne, ny, half, width = dims
    rows = ne * half
    sub = rows // 2
    pipe = lax.axis_index("pipe")
    e = lax.axis_index("expert")
    y = pipe // 2
    c = pipe % 2
    right = {"pipe": (y + 1) % ny * 2 + c}
    left = {"pipe": (y + ny - 1) % ny * 2 + c}
    peer = {"pipe": 2 * y + 1 - c}
    far = ny // 2
    hop = far - 1

    def chunk(j):
        return (y + j + ny) % ny

    def at16(x):
        return pl.multiple_of(x, 16)

    def remote(src, dst, send, recv, device):
        return pltpu.make_async_remote_copy(
            src_ref=src, dst_ref=dst, send_sem=send, recv_sem=recv, device_id=device, device_id_type=MESH
        )

    sent = []

    def go(copy):
        copy.start()
        sent.append(copy)

    barrier = pltpu.get_barrier_semaphore()
    for device in [{"expert": (e + j) % ne} for j in range(1, ne)] + [right, left, peer]:
        pl.semaphore_signal(barrier, inc=1, device_id=device, device_id_type=MESH)

    loads = []
    for i, j in enumerate((0, far)):
        cols = pl.ds(pl.multiple_of(chunk(j) * width, 128), width)
        loads.append(pltpu.make_async_copy(tokens.at[:, cols], tok_v.at[i], load_sem.at[i]))
    for i, (src, dst) in enumerate(((wg, wg_v), (wu, wu_v), (wd, wd_v))):
        loads.append(pltpu.make_async_copy(src.at[0], dst, load_sem.at[2 + i]))
    for copy in loads:
        copy.start()

    toks = routes.shape[0]
    lane = lax.broadcasted_iota(jnp.int32, (toks, 2 * rows), 1)
    hbits, rbits = half.bit_length() - 1, rows.bit_length() - 1
    expert_of = (lane >> hbits) & (ne - 1)
    slot_of = ((lane >> rbits) << hbits) + (lane & (half - 1))
    first = routes[:, 0:1] == expert_of
    second = routes[:, 1:2] == expert_of
    named = jnp.logical_or(first, second)
    before = (
        lax.broadcasted_iota(jnp.int32, (toks, toks), 0) > lax.broadcasted_iota(jnp.int32, (toks, toks), 1)
    ).astype(F32)
    rank = jnp.dot(before.astype(BF16), named.astype(F32).astype(BF16), preferred_element_type=F32)
    taken = jnp.logical_and(named, rank == slot_of.astype(F32))
    mix[...] = jnp.where(taken, jnp.where(first, route_w[:, 0:1], route_w[:, 1:2]), 0.0)
    picked = taken.astype(F32)
    mine = jnp.where(c == 0, picked[:, :rows], picked[:, rows:]).astype(BF16)
    for i in range(2):
        loads[i].wait()
        xs[i] = lax.dot_general(
            mine, tok_v[i], (((0,), (0,)), ((), ())), preferred_element_type=F32
        ).astype(BF16)

    pl.semaphore_wait(barrier, ne - 1 + 3)

    own_rows = pl.ds(at16(c * rows + e * half), half)
    for i, j, send, recv in ((0, 0, xs_sem, xr_sem), (1, far, os_sem, or_sem)):
        for n in range(1, ne):
            t = (e + n) % ne
            go(
                remote(
                    xs.at[i, pl.ds(at16(t * half), half)],
                    xbuf.at[chunk(j), own_rows],
                    send.at[n],
                    recv.at[n],
                    {"expert": t},
                )
            )
        xbuf[chunk(j), own_rows, :] = xs[i, pl.ds(at16(e * half), half), :]

    def x_arrived(i, j, send, recv):
        for n in range(1, ne):
            s = (e + ne - n) % ne
            where = pl.ds(at16(c * rows + s * half), half)
            remote(xs.at[i, pl.ds(0, half)], xbuf.at[chunk(j), where], send.at[n], recv.at[n], {"expert": s}).wait_recv()

    def piece(b):
        return pl.ds(at16(c * rows + b * sub), sub)

    def y_copy(way, s, b):
        j = -s if way == 0 else s
        ref = xbuf.at[chunk(j), piece(b)]
        return remote(ref, ref, ys_sem.at[way, s, b], yr_sem.at[way, s, b], right if way == 0 else left)

    def y_arrived(way, s, b):
        j = -1 - s if way == 0 else s + 1
        ref = xbuf.at[chunk(j), piece(b)]
        remote(ref, ref, ys_sem.at[way, s, b], yr_sem.at[way, s, b], right if way == 0 else left).wait_recv()

    def share(j):
        ref = xbuf.at[chunk(j), pl.ds(at16(c * rows), rows)]
        return remote(ref, ref, cs_sem.at[j + hop], cr_sem.at[j + hop], peer)

    def shared(j):
        ref = xbuf.at[chunk(j), pl.ds(at16((1 - c) * rows), rows)]
        remote(ref, ref, cs_sem.at[j + hop], cr_sem.at[j + hop], peer).wait_recv()

    def gemm(j, start=False):
        k = chunk(j)
        shared(j)
        lhs = xbuf[k]
        deep = pl.ds(pl.multiple_of(k * width, 128), width)
        for acc, w in ((acc_g, wg_v), (acc_u, wu_v)):
            term = jnp.dot(lhs, w[deep, :], preferred_element_type=F32)
            acc[...] = term if start else acc[...] + term

    x_arrived(0, 0, xs_sem, xr_sem)
    for b in range(2):
        for way in range(2):
            go(y_copy(way, 0, b))
    go(share(0))
    loads[2].wait()
    loads[3].wait()
    gemm(0, True)
    for s in range(hop):
        for b in range(2):
            for way in range(2):
                y_arrived(way, s, b)
                if s + 1 < hop:
                    go(y_copy(way, s + 1, b))
        go(share(-1 - s))
        go(share(s + 1))
        if s == 0:
            x_arrived(1, far, os_sem, or_sem)
            go(share(far))
            gemm(far)
        gemm(-1 - s)
        gemm(s + 1)

    gate = acc_g[...]
    hid[...] = (gate / (1.0 + jnp.exp(-gate)) * acc_u[...]).astype(BF16)
    loads[4].wait()

    low = lax.broadcasted_iota(jnp.int32, (rows, width), 1) < width // 2

    def down(j):
        i = j + hop
        cols = pl.ds(pl.multiple_of(chunk(j) * width, 128), width)
        part = jnp.dot(hid[...], wd_v[:, cols], preferred_element_type=F32)
        a, b = part[:rows], part[rows:]
        pk[i, 0] = jnp.where(low, a, pltpu.roll(b, width // 2, 1)).astype(BF16)
        pk[i, 1] = jnp.where(low, pltpu.roll(a, width // 2, 1), b).astype(BF16)
        go(remote(pk.at[i, 1 - c], cin.at[i], ds_sem.at[i], dr_sem.at[i], peer))

    def met(j):
        i = j + hop
        remote(pk.at[i, 1 - c], cin.at[i], ds_sem.at[i], dr_sem.at[i], peer).wait_recv()

    def own(j, b):
        i = j + hop
        at = pl.ds(b * sub, sub)
        return pk[i, c, at, :].astype(F32) + cin[i, at, :].astype(F32)

    def r_copy(way, s, b):
        at = pl.ds(b * sub, sub)
        return remote(
            rout.at[way, s, at],
            rin.at[way, s, at],
            rs_sem.at[way, s, b],
            rr_sem.at[way, s, b],
            right if way == 0 else left,
        )

    def got(way, s, b):
        r_copy(way, s, b).wait_recv()
        return rin[way, s, pl.ds(b * sub, sub), :].astype(F32)

    def pass_on(way, s, b):
        if s == 0:
            total = own(far, b)
        else:
            total = own(far - s if way == 0 else s - far, b)
            if s > 1 or b == way:
                total = total + got(way, s - 1, b)
        rout[way, s, pl.ds(b * sub, sub), :] = total.astype(BF16)
        go(r_copy(way, s, b))

    down(far)
    down(far - 1)
    down(1 - far)
    met(far)
    pass_on(0, 0, 0)
    pass_on(1, 0, 1)
    met(far - 1)
    pass_on(0, 1, 1)
    met(1 - far)
    pass_on(1, 1, 0)
    for j in range(far - 2, 0, -1):
        down(j)
        down(-j)
    down(0)
    pass_on(0, 1, 0)
    pass_on(1, 1, 1)
    for s in range(2, far):
        met(far - s)
        met(s - far)
        for b in (1, 0):
            pass_on(0, s, b)
            pass_on(1, s, 1 - b)
    met(0)
    for b in range(2):
        total = own(0, b) + got(0, far - 1, b) + got(1, far - 1, b)
        fin[pl.ds(b * sub, sub), :] = total.astype(BF16)

    for n in range(1, ne):
        t = (e + n) % ne
        go(
            remote(
                fin.at[pl.ds(at16(t * half), half)],
                rbuf.at[pl.ds(at16(e * half), half)],
                fs_sem.at[n],
                fr_sem.at[n],
                {"expert": t},
            )
        )
    rbuf[pl.ds(at16(e * half), half), :] = fin[pl.ds(at16(e * half), half), :]
    hi = mix[...].astype(BF16)
    lo = (mix[...] - hi.astype(F32)).astype(BF16)
    for n in range(1, ne):
        s = (e + ne - n) % ne
        remote(
            fin.at[pl.ds(0, half)], rbuf.at[pl.ds(at16(s * half), half)], fs_sem.at[n], fr_sem.at[n], {"expert": s}
        ).wait_recv()
    back = rbuf[...]

    def mixed(side):
        cols = slice(side * rows, side * rows + rows)
        return jnp.dot(hi[:, cols], back, preferred_element_type=F32) + jnp.dot(
            lo[:, cols], back, preferred_element_type=F32
        )

    total = mixed(0) + pltpu.roll(mixed(1), width // 2, 1)
    out[...] = total[:, : width // 2].astype(BF16)
    for copy in sent:
        copy.wait_send()


def on_device(tokens, routes, route_weights, w_gate, w_up, w_down):
    ne = lax.axis_size("expert")
    ny = lax.axis_size("pipe") // 2
    toks, model = tokens.shape
    hidden = w_gate.shape[2]
    width = model // ny
    half = 16
    rows = ne * half
    far = ny // 2
    vmem = pl.BlockSpec(memory_space=pltpu.VMEM)
    hbm = pl.BlockSpec(memory_space=pl.ANY)
    dma = pltpu.SemaphoreType.DMA
    return pl.pallas_call(
        functools.partial(kernel, (ne, ny, half, width)),
        out_shape=jax.ShapeDtypeStruct((toks, width // 2), BF16),
        in_specs=[hbm, vmem, vmem, hbm, hbm, hbm],
        out_specs=vmem,
        scratch_shapes=[
            pltpu.VMEM((2, toks, width), BF16),
            pltpu.VMEM((2, rows, width), BF16),
            pltpu.VMEM((ny, 2 * rows, width), BF16),
            pltpu.VMEM((model, hidden), BF16),
            pltpu.VMEM((model, hidden), BF16),
            pltpu.VMEM((hidden, model), BF16),
            pltpu.VMEM((2 * rows, hidden), F32),
            pltpu.VMEM((2 * rows, hidden), F32),
            pltpu.VMEM((2 * rows, hidden), BF16),
            pltpu.VMEM((toks, 2 * rows), F32),
            pltpu.VMEM((ny, 2, rows, width), BF16),
            pltpu.VMEM((ny, rows, width), BF16),
            pltpu.VMEM((2, far, rows, width), BF16),
            pltpu.VMEM((2, far, rows, width), BF16),
            pltpu.VMEM((rows, width), BF16),
            pltpu.VMEM((rows, width), BF16),
            dma((5,)),
            dma((ne,)),
            dma((ne,)),
            dma((ne,)),
            dma((ne,)),
            dma((2, far, 2)),
            dma((2, far, 2)),
            dma((ny,)),
            dma((ny,)),
            dma((ny,)),
            dma((ny,)),
            dma((2, far, 2)),
            dma((2, far, 2)),
            dma((ne,)),
            dma((ne,)),
        ],
        compiler_params=pltpu.CompilerParams(
            collective_id=0, has_side_effects=True, vmem_limit_bytes=40 * 1024 * 1024
        ),
    )(tokens, routes, route_weights, w_gate, w_up, w_down)


def solution(mesh):
    return jax.shard_map(
        on_device,
        mesh=mesh,
        in_specs=(
            P(("dp", "expert"), None),
            P(("dp", "expert"), None),
            P(("dp", "expert"), None),
            P("expert", None, "pipe"),
            P("expert", None, "pipe"),
            P("expert", "pipe", None),
        ),
        out_specs=P(("dp", "expert"), "pipe"),
        check_vma=False,
    )
```

time: 174 us -> 63.8 us (0.37)
  the two profiles are of different devices: /device:TPU:1 before, /device:TPU:20 now
where the time goes in v1:
time: 63.8 us; the launch traced here: 63.5 us
  Pallas kernels  54.5 us (85%)
  local copies, waits for them, and re-layouts  8.9 us (14%)
    pallas_call x1, Pallas kernels, on_device(): pl.pallas_call(functools.partial(kernel, (ne, ny, half, width)), out_shap...  54.5 us
    unnamed x11, local copies, waits for them, and re-layouts  8.9 us

profile of v1, /device:TPU:20, one launch (start us, length us, event | category | flops | bytes accessed | tf_op | source)
XLA Modules:
  0.0 63.5 jit_solution(6205066580906758255)
XLA Ops:
  0.0 0.8 %copy.7.routes = s32[96,2]{1,0:T(8,128)S(1)} copy(s32[96,2]{0,1:T(2,128)} %param.7) | data formatting | bytes 1536 | tf_op args[1]
  0.8 0.8 %copy.8.route_w = f32[96,2]{1,0:T(8,128)S(1)} copy(f32[96,2]{0,1:T(2,128)} %param.8) | data formatting | bytes 1536 | tf_op args[2]
  1.6 0.0 copy-start
  1.6 1.9 %copy-done = bf16[1,3072,512]{2,1,0:T(8,128)(2,1)S(1)} copy-done((bf16[1,3072,512]{2,1,0:T(8,128)(2,1)S(1)}, bf16[1,3072,512]{2,1,0:T(8,128)(2,1)}, u32[]{:S(2)}) %copy-start) | copy-done | bytes 3145752
  3.4 0.0 copy-start.1
  3.4 1.9 %copy-done.1 = bf16[1,3072,512]{2,1,0:T(8,128)(2,1)S(1)} copy-done((bf16[1,3072,512]{2,1,0:T(8,128)(2,1)S(1)}, bf16[1,3072,512]{2,1,0:T(8,128)(2,1)}, u32[]{:S(2)}) %copy-start.1) | copy-done | bytes 3145752
  5.3 0.0 copy-start.2
  5.3 1.9 %copy-done.2 = bf16[1,512,3072]{2,1,0:T(8,128)(2,1)S(1)} copy-done((bf16[1,512,3072]{2,1,0:T(8,128)(2,1)S(1)}, bf16[1,512,3072]{2,1,0:T(8,128)(2,1)}, u32[]{:S(2)}) %copy-start.2) | copy-done | bytes 3145752
  7.2 0.0 copy-start.3
  7.2 1.1 %copy-done.3 = bf16[96,3072]{1,0:T(8,128)(2,1)S(1)} copy-done((bf16[96,3072]{1,0:T(8,128)(2,1)S(1)}, bf16[96,3072]{1,0:T(8,128)(2,1)}, u32[]{:S(2)}) %copy-start.3) | copy-done | bytes 589848
  8.3 54.5 %shard_map.64 = bf16[96,192]{1,0:T(8,128)(2,1)S(1)} custom-call(bf16[96,3072]{1,0:T(8,128)(2,1)S(1)} %copy-done.3, s32[96,2]{1,0:T(8,128)S(1)} %copy.7.routes, f32[96,2]{1,0:T(8,128)S(1)} %copy.8.route_w, bf16[1,3072,512]{2,1,0:T(8,128)(2,1)S(1)} %copy-done, bf16[1,3072,512]{2,1,0:T(8,128)(2,1)S(1)} %copy-done.1, bf16[1,512,3072]{2,1,0:T(8,128)(2,1)S(1)} %copy-done.2), custom_call_target="tpu_custom_call" | custom-call | tf_op jit(solution)/shard_map/pallas_call | solution.py:317
  62.8 0.6 copy.10
Async XLA Ops:
  1.6 1.9 %copy-start = (bf16[1,3072,512]{2,1,0:T(8,128)(2,1)S(1)}, bf16[1,3072,512]{2,1,0:T(8,128)(2,1)}, u32[]{:S(2)}) copy-start(bf16[1,3072,512]{2,1,0:T(8,128)(2,1)} %wg.1) | copy-start | bytes 9437188
  3.4 1.9 %copy-start.1 = (bf16[1,3072,512]{2,1,0:T(8,128)(2,1)S(1)}, bf16[1,3072,512]{2,1,0:T(8,128)(2,1)}, u32[]{:S(2)}) copy-start(bf16[1,3072,512]{2,1,0:T(8,128)(2,1)} %wu.1) | copy-start | bytes 9437188
  5.3 1.9 %copy-start.2 = (bf16[1,512,3072]{2,1,0:T(8,128)(2,1)S(1)}, bf16[1,512,3072]{2,1,0:T(8,128)(2,1)}, u32[]{:S(2)}) copy-start(bf16[1,512,3072]{2,1,0:T(8,128)(2,1)} %wd.1) | copy-start | bytes 9437188
  7.2 1.1 %copy-start.3 = (bf16[96,3072]{1,0:T(8,128)(2,1)S(1)}, bf16[96,3072]{1,0:T(8,128)(2,1)}, u32[]{:S(2)}) copy-start(bf16[96,3072]{1,0:T(8,128)(2,1)} %tokens.1) | copy-start | bytes 1769476

commit v2 on v1

v2 whole, which is shorter than its diff:
```python
import functools

import jax
import jax.numpy as jnp
from jax import lax
from jax.experimental import pallas as pl
from jax.experimental.pallas import tpu as pltpu
from jax.sharding import PartitionSpec as P

MESH = pl.DeviceIdType.MESH
F32 = jnp.float32
BF16 = jnp.bfloat16


def kernel(
    dims,
    tokens,
    routes,
    route_w,
    wg,
    wu,
    wd,
    out,
    route_v,
    weight_v,
    tok_v,
    xs,
    xbuf,
    wg_v,
    wu_v,
    wd_v,
    acc_g,
    acc_u,
    hid,
    mix,
    pk,
    cin,
    rin,
    rout,
    fin,
    rbuf,
    load_sem,
    xs_sem,
    xr_sem,
    os_sem,
    or_sem,
    ys_sem,
    yr_sem,
    cs_sem,
    cr_sem,
    ds_sem,
    dr_sem,
    rs_sem,
    rr_sem,
    fs_sem,
    fr_sem,
):
    ne, ny, half, width = dims
    rows = ne * half
    parts = 4
    sub = rows // parts
    pipe = lax.axis_index("pipe")
    e = lax.axis_index("expert")
    y = pipe // 2
    c = pipe % 2
    right = {"pipe": (y + 1) % ny * 2 + c}
    left = {"pipe": (y + ny - 1) % ny * 2 + c}
    peer = {"pipe": 2 * y + 1 - c}
    far = ny // 2
    hop = far - 1

    def chunk(j):
        return (y + j + ny) % ny

    def at16(x):
        return pl.multiple_of(x, 16)

    def remote(src, dst, send, recv, device):
        return pltpu.make_async_remote_copy(
            src_ref=src, dst_ref=dst, send_sem=send, recv_sem=recv, device_id=device, device_id_type=MESH
        )

    sent = []

    def go(copy):
        copy.start()
        sent.append(copy)

    barrier = pltpu.get_barrier_semaphore()
    for device in [{"expert": (e + j) % ne} for j in range(1, ne)] + [right, left, peer]:
        pl.semaphore_signal(barrier, inc=1, device_id=device, device_id_type=MESH)

    pairs = [(routes, route_v), (route_w, weight_v)]
    for i, j in enumerate((0, far)):
        cols = pl.ds(pl.multiple_of(chunk(j) * width, 128), width)
        pairs.append((tokens.at[:, cols], tok_v.at[i]))
    pairs += [(wg.at[0], wg_v), (wu.at[0], wu_v), (wd.at[0], wd_v)]
    loads = [pltpu.make_async_copy(src, dst, load_sem.at[i]) for i, (src, dst) in enumerate(pairs)]
    for copy in loads:
        copy.start()

    toks = tok_v.shape[1]
    row = lax.broadcasted_iota(jnp.int32, (2 * rows, toks), 0)
    hbits, rbits = half.bit_length() - 1, rows.bit_length() - 1
    expert_of = (row >> hbits) & (ne - 1)
    slot_of = ((row >> rbits) << hbits) + (row & (half - 1))
    loads[0].wait()
    loads[1].wait()
    first = route_v[0:1, :] == expert_of
    second = route_v[1:2, :] == expert_of
    named = jnp.logical_or(first, second)
    before = (
        lax.broadcasted_iota(jnp.int32, (toks, toks), 0) < lax.broadcasted_iota(jnp.int32, (toks, toks), 1)
    ).astype(F32)
    rank = jnp.dot(named.astype(F32).astype(BF16), before.astype(BF16), preferred_element_type=F32)
    taken = jnp.logical_and(named, rank == slot_of.astype(F32))
    mix[...] = jnp.where(taken, jnp.where(first, weight_v[0:1, :], weight_v[1:2, :]), 0.0)
    picked = taken.astype(F32)
    mine = jnp.where(c == 0, picked[:rows], picked[rows:]).astype(BF16)
    for i in range(2):
        loads[2 + i].wait()
        xs[i] = jnp.dot(mine, tok_v[i], preferred_element_type=F32).astype(BF16)

    pl.semaphore_wait(barrier, ne - 1 + 3)

    own_rows = pl.ds(at16(c * rows + e * half), half)
    far_first = sorted(range(1, ne), key=lambda n: -min(n, ne - n))
    for i, j, send, recv in ((0, 0, xs_sem, xr_sem), (1, far, os_sem, or_sem)):
        for n in far_first:
            t = (e + n) % ne
            go(
                remote(
                    xs.at[i, pl.ds(at16(t * half), half)],
                    xbuf.at[chunk(j), own_rows],
                    send.at[n],
                    recv.at[n],
                    {"expert": t},
                )
            )
        xbuf[chunk(j), own_rows, :] = xs[i, pl.ds(at16(e * half), half), :]

    def x_arrived(i, j, send, recv):
        for n in reversed(far_first):
            s = (e + ne - n) % ne
            where = pl.ds(at16(c * rows + s * half), half)
            remote(xs.at[i, pl.ds(0, half)], xbuf.at[chunk(j), where], send.at[n], recv.at[n], {"expert": s}).wait_recv()

    def y_copy(way, s, b, arriving=False):
        j = s + 1 if arriving else s
        ref = xbuf.at[chunk(-j if way == 0 else j), pl.ds(at16(c * rows + b * sub), sub)]
        return remote(ref, ref, ys_sem.at[way, s, b], yr_sem.at[way, s, b], right if way == 0 else left)

    def share(j, b=0, n=parts, core=c):
        i = j + hop
        ref = xbuf.at[chunk(j), pl.ds(at16(core * rows + b * sub), n * sub)]
        return remote(ref, ref, cs_sem.at[i, b], cr_sem.at[i, b], peer)

    def gemm(j, start=False):
        k = chunk(j)
        if hop == abs(j):
            for b in range(parts):
                share(j, b, 1, 1 - c).wait_recv()
        else:
            share(j, core=1 - c).wait_recv()
        lhs = xbuf[k]
        deep = pl.ds(pl.multiple_of(k * width, 128), width)
        for acc, w in ((acc_g, wg_v), (acc_u, wu_v)):
            term = jnp.dot(lhs, w[deep, :], preferred_element_type=F32)
            acc[...] = term if start else acc[...] + term

    x_arrived(0, 0, xs_sem, xr_sem)
    for b in range(parts):
        for way in range(2):
            go(y_copy(way, 0, b))
    go(share(0))
    for s in range(hop):
        for b in range(parts):
            for way in range(2):
                y_copy(way, s, b, True).wait_recv()
                if s + 1 < hop:
                    go(y_copy(way, s + 1, b))
                else:
                    go(share(-hop if way == 0 else hop, b, 1))
        if s + 1 < hop:
            go(share(-1 - s))
            go(share(s + 1))
        if s == 0:
            loads[4].wait()
            loads[5].wait()
            gemm(0, True)
        if s == 1:
            x_arrived(1, far, os_sem, or_sem)
            go(share(far))
        if s > 0:
            gemm(-s)
            gemm(s)
    gemm(far)
    gemm(-hop)
    gemm(hop)

    gate = acc_g[...]
    hid[...] = (gate / (1.0 + jnp.exp(-gate)) * acc_u[...]).astype(BF16)
    loads[6].wait()

    low = lax.broadcasted_iota(jnp.int32, (rows, width), 1) < width // 2

    def down(j):
        i = j + hop
        cols = pl.ds(pl.multiple_of(chunk(j) * width, 128), width)
        part = jnp.dot(hid[...], wd_v[:, cols], preferred_element_type=F32)
        a, b = part[:rows], part[rows:]
        pk[i, 0] = jnp.where(low, a, pltpu.roll(b, width // 2, 1)).astype(BF16)
        pk[i, 1] = jnp.where(low, pltpu.roll(a, width // 2, 1), b).astype(BF16)
        go(remote(pk.at[i, 1 - c], cin.at[i], ds_sem.at[i], dr_sem.at[i], peer))

    def met(j):
        i = j + hop
        remote(pk.at[i, 1 - c], cin.at[i], ds_sem.at[i], dr_sem.at[i], peer).wait_recv()

    def own(j, b):
        i = j + hop
        at = pl.ds(b * sub, sub)
        return pk[i, c, at, :].astype(F32) + cin[i, at, :].astype(F32)

    def r_copy(way, s, b):
        at = pl.ds(b * sub, sub)
        return remote(
            rout.at[way, s, at],
            rin.at[way, s, at],
            rs_sem.at[way, s, b],
            rr_sem.at[way, s, b],
            right if way == 0 else left,
        )

    def got(way, s, b):
        r_copy(way, s, b).wait_recv()
        return rin[way, s, pl.ds(b * sub, sub), :].astype(F32)

    def pass_on(way, s, b):
        if s == 0:
            total = own(far, b)
        else:
            total = own(far - s if way == 0 else s - far, b)
            if s > 1 or b // (parts // 2) == way:
                total = total + got(way, s - 1, b)
        rout[way, s, pl.ds(b * sub, sub), :] = total.astype(BF16)
        go(r_copy(way, s, b))

    down(far)
    for j in range(far - 1, max(0, far - 3), -1):
        down(j)
        down(-j)
    early, late = range(parts // 2), range(parts // 2, parts)
    met(far)
    for b in early:
        pass_on(0, 0, b)
        pass_on(1, 0, parts - 1 - b)
    met(far - 1)
    met(1 - far)
    for b in late:
        pass_on(0, 1, b)
        pass_on(1, 1, parts - 1 - b)
    for j in range(far - 3, 0, -1):
        down(j)
        down(-j)
    down(0)
    for b in early:
        pass_on(0, 1, b)
        pass_on(1, 1, parts - 1 - b)
    for s in range(2, far):
        met(far - s)
        met(s - far)
        for b in (*late, *early):
            pass_on(0, s, b)
            pass_on(1, s, parts - 1 - b)
    met(0)

    per = ne // parts
    own_back = pl.ds(at16(e * half), half)

    def back_copy(t):
        return remote(
            fin.at[pl.ds(t * half, half)], rbuf.at[own_back], fs_sem.at[t], fr_sem.at[e], {"expert": t}
        )

    order = [b for pair in zip(late, reversed(early)) for b in pair]
    for b in order:
        total = own(0, b) + got(0, far - 1, b) + got(1, far - 1, b)
        fin[pl.ds(b * sub, sub), :] = total.astype(BF16)
        for t in range(b * per, b * per + per):

            @pl.when(t != e)
            def _():
                back_copy(t).start()

    rbuf[own_back, :] = fin[own_back, :]
    weights = mix[...].T
    hi = weights.astype(BF16)
    lo = (weights - hi.astype(F32)).astype(BF16)
    for n in range(1, ne):
        t = (e + n) % ne
        at = pl.ds(at16(t * half), half)
        remote(fin.at[at], rbuf.at[at], fs_sem.at[t], fr_sem.at[t], {"expert": t}).wait()
    back = rbuf[...]

    def mixed(side):
        cols = slice(side * rows, side * rows + rows)
        return jnp.dot(hi[:, cols], back, preferred_element_type=F32) + jnp.dot(
            lo[:, cols], back, preferred_element_type=F32
        )

    total = mixed(0) + pltpu.roll(mixed(1), width // 2, 1)
    out[...] = total[:, : width // 2].astype(BF16)
    for copy in sent:
        copy.wait_send()


def on_device(tokens, routes, route_weights, w_gate, w_up, w_down):
    ne = lax.axis_size("expert")
    ny = lax.axis_size("pipe") // 2
    toks, model = tokens.shape
    hidden = w_gate.shape[2]
    width = model // ny
    half = 16
    rows = ne * half
    far = ny // 2
    vmem = pl.BlockSpec(memory_space=pltpu.VMEM)
    hbm = pl.BlockSpec(memory_space=pl.ANY)
    dma = pltpu.SemaphoreType.DMA
    return pl.pallas_call(
        functools.partial(kernel, (ne, ny, half, width)),
        out_shape=jax.ShapeDtypeStruct((toks, width // 2), BF16),
        in_specs=[hbm] * 6,
        out_specs=vmem,
        scratch_shapes=[
            pltpu.VMEM((2, toks), jnp.int32),
            pltpu.VMEM((2, toks), F32),
            pltpu.VMEM((2, toks, width), BF16),
            pltpu.VMEM((2, rows, width), BF16),
            pltpu.VMEM((ny, 2 * rows, width), BF16),
            pltpu.VMEM((model, hidden), BF16),
            pltpu.VMEM((model, hidden), BF16),
            pltpu.VMEM((hidden, model), BF16),
            pltpu.VMEM((2 * rows, hidden), F32),
            pltpu.VMEM((2 * rows, hidden), F32),
            pltpu.VMEM((2 * rows, hidden), BF16),
            pltpu.VMEM((2 * rows, toks), F32),
            pltpu.VMEM((ny, 2, rows, width), BF16),
            pltpu.VMEM((ny, rows, width), BF16),
            pltpu.VMEM((2, far, rows, width), BF16),
            pltpu.VMEM((2, far, rows, width), BF16),
            pltpu.VMEM((rows, width), BF16),
            pltpu.VMEM((rows, width), BF16),
            dma((7,)),
            dma((ne,)),
            dma((ne,)),
            dma((ne,)),
            dma((ne,)),
            dma((2, far, 4)),
            dma((2, far, 4)),
            dma((ny, 4)),
            dma((ny, 4)),
            dma((ny,)),
            dma((ny,)),
            dma((2, far, 4)),
            dma((2, far, 4)),
            dma((ne,)),
            dma((ne,)),
        ],
        compiler_params=pltpu.CompilerParams(
            collective_id=0, has_side_effects=True, vmem_limit_bytes=60 * 1024 * 1024
        ),
    )(tokens, routes.T, route_weights.T, w_gate, w_up, w_down)


def solution(mesh):
    return jax.shard_map(
        on_device,
        mesh=mesh,
        in_specs=(
            P(("dp", "expert"), None),
            P(("dp", "expert"), None),
            P(("dp", "expert"), None),
            P("expert", None, "pipe"),
            P("expert", None, "pipe"),
            P("expert", "pipe", None),
        ),
        out_specs=P(("dp", "expert"), "pipe"),
        check_vma=False,
    )
```

time: 63.8 us -> 58.2 us (0.912)
  the two profiles are of different devices: /device:TPU:20 before, /device:TPU:2 now
where the time goes in v2:
time: 58.2 us; the launch traced here: 58 us
  Pallas kernels  56.6 us (97%)
  local copies, waits for them, and re-layouts  1.42 us (2%)
    pallas_call x1, Pallas kernels, on_device(): pl.pallas_call(functools.partial(kernel, (ne, ny, half, width)), out_shap...  56.6 us
    unnamed x1, local copies, waits for them, and re-layouts  1.42 us

profile of v2, /device:TPU:2, one launch (start us, length us, event | category | flops | bytes accessed | tf_op | source)
XLA Modules:
  0.0 58.0 jit_solution(12266329369864708610)
XLA Ops:
  0.0 56.6 %shard_map.64 = bf16[96,192]{1,0:T(8,128)(2,1)} custom-call(bf16[96,3072]{1,0:T(8,128)(2,1)} %tokens.1, s32[2,96]{1,0:T(2,128)} %bitcast.2, f32[2,96]{1,0:T(2,128)} %bitcast.3, bf16[1,3072,512]{2,1,0:T(8,128)(2,1)} %wg.1, bf16[1,3072,512]{2,1,0:T(8,128)(2,1)} %wu.1, bf16[1,512,3072]{2,1,0:T(8,128)(2,1)} %wd.1), custom_call_target="tpu_custom_call" | custom-call | tf_op jit(solution)/shard_map/pallas_call | solution.py:330
  56.6 1.4 %copy.8 = bf16[96,192]{1,0:T(8,128)(2,1)} copy(bf16[96,192]{1,0:T(8,128)(2,1)} %shard_map.64) | data formatting | bytes 73728

commit v3 on v2

--- a/solution.py
+++ b/solution.py
@@ -42,8 +42,6 @@
     load_sem,
     xs_sem,
     xr_sem,
-    os_sem,
-    or_sem,
     ys_sem,
     yr_sem,
     cs_sem,
@@ -54,6 +52,7 @@
     rr_sem,
     fs_sem,
     fr_sem,
+    ready,
 ):
     ne, ny, half, width = dims
     rows = ne * half
@@ -63,11 +62,36 @@
     e = lax.axis_index("expert")
     y = pipe // 2
     c = pipe % 2
+    d = lax.axis_index("dp")
+    far = ny // 2
+    hop = far - 1
+    steps = far - 2
+
+    def zero(v, n):
+        return 1 - (v + n - 1) // n
+
+    def carrier(at_y, at_e, h):
+        if h == 1:
+            return 1
+        return zero(d, lax.axis_size("dp")) * zero(at_y, ny) * zero(at_e, ne)
+
+    def chip(at_y, h):
+        at_y = (at_y + ny) % ny
+        return {"pipe": 2 * at_y + carrier(at_y, e, h)}
+
+    def across(t, h):
+        return {"pipe": 2 * y + carrier(y, t, h), "expert": t}
+
     right = {"pipe": (y + 1) % ny * 2 + c}
     left = {"pipe": (y + ny - 1) % ny * 2 + c}
     peer = {"pipe": 2 * y + 1 - c}
-    far = ny // 2
-    hop = far - 1
+    front = d == 0
+    lone = jnp.logical_and(front, jnp.logical_and(pipe == 0, e == 0))
+    double = jnp.logical_and(front, jnp.logical_and(pipe == 1, e == 0))
+    in_row = jnp.logical_and(y == 0, e != 0)
+    in_column = jnp.logical_and(e == 0, jnp.logical_or(y == 1, y == ny - 1))
+    beside = jnp.logical_and(jnp.logical_and(front, c == 0), jnp.logical_or(in_row, in_column))
+    active = [carrier(y, e, h) == c for h in range(2)]
 
     def chunk(j):
         return (y + j + ny) % ny
@@ -81,17 +105,47 @@
         )
 
     sent = []
+    sent_of = [[], []]
 
     def go(copy):
         copy.start()
         sent.append(copy)
 
+    def send(h, make):
+        make().start()
+        sent_of[h].append(make)
+
+    def carry(work):
+        for h in range(2):
+
+            @pl.when(active[h])
+            def _():
+                work(h)
+
     barrier = pltpu.get_barrier_semaphore()
-    for device in [{"expert": (e + j) % ne} for j in range(1, ne)] + [right, left, peer]:
-        pl.semaphore_signal(barrier, inc=1, device_id=device, device_id_type=MESH)
+
+    def greet(semaphore, device):
+        pl.semaphore_signal(semaphore, inc=1, device_id=device, device_id_type=MESH)
+
+    neighbours = [{"expert": (e + j) % ne} for j in range(1, ne)] + [right, left, peer]
+
+    @pl.when(jnp.logical_not(lone))
+    def _():
+        for device in neighbours:
+            greet(barrier, device)
+
+    @pl.when(double)
+    def _():
+        for device in [{"pipe": 0, "expert": t} for t in range(1, ne)] + [{"pipe": 2}, {"pipe": 2 * ny - 2}]:
+            greet(barrier, device)
+
+    @pl.when(beside)
+    def _():
+        greet(barrier, {"pipe": 1, "expert": 0})
 
     pairs = [(routes, route_v), (route_w, weight_v)]
-    for i, j in enumerate((0, far)):
+    direct = [0, far] + [j for k in range(steps + 1, far) for j in (-k, k)]
+    for i, j in enumerate(direct):
         cols = pl.ds(pl.multiple_of(chunk(j) * width, 128), width)
         pairs.append((tokens.at[:, cols], tok_v.at[i]))
     pairs += [(wg.at[0], wg_v), (wu.at[0], wu_v), (wd.at[0], wd_v)]
@@ -116,91 +170,155 @@
     taken = jnp.logical_and(named, rank == slot_of.astype(F32))
     mix[...] = jnp.where(taken, jnp.where(first, weight_v[0:1, :], weight_v[1:2, :]), 0.0)
     picked = taken.astype(F32)
-    mine = jnp.where(c == 0, picked[:rows], picked[rows:]).astype(BF16)
-    for i in range(2):
-        loads[2 + i].wait()
-        xs[i] = jnp.dot(mine, tok_v[i], preferred_element_type=F32).astype(BF16)
-
-    pl.semaphore_wait(barrier, ne - 1 + 3)
-
-    own_rows = pl.ds(at16(c * rows + e * half), half)
+    picked = picked.astype(BF16)
+    loads[2].wait()
+    xs[0] = jnp.dot(picked, tok_v[0], preferred_element_type=F32).astype(BF16)
+
+    @pl.when(jnp.logical_not(double))
+    def _():
+        pl.semaphore_wait(barrier, len(neighbours))
+
+    @pl.when(double)
+    def _():
+        pl.semaphore_wait(barrier, 2 * len(neighbours) - 2)
+
+    @pl.when(lone)
+    def _():
+        for device in neighbours:
+            greet(ready, device)
+
     far_first = sorted(range(1, ne), key=lambda n: -min(n, ne - n))
-    for i, j, send, recv in ((0, 0, xs_sem, xr_sem), (1, far, os_sem, or_sem)):
+
+    def slab(core, t):
+        return pl.ds(at16(core * rows + t * half), half)
+
+    def x_copy(h, i, n):
+        t = (e + n) % ne
+        return remote(
+            xs.at[i, slab(h, t)],
+            xbuf.at[chunk(direct[i]), slab(h, e)],
+            xs_sem.at[h, i, n],
+            xr_sem.at[h, i, n],
+            across(t, h),
+        )
+
+    def x_send(h, i):
         for n in far_first:
-            t = (e + n) % ne
-            go(
-                remote(
-                    xs.at[i, pl.ds(at16(t * half), half)],
-                    xbuf.at[chunk(j), own_rows],
-                    send.at[n],
-                    recv.at[n],
-                    {"expert": t},
-                )
-            )
-        xbuf[chunk(j), own_rows, :] = xs[i, pl.ds(at16(e * half), half), :]
-
-    def x_arrived(i, j, send, recv):
+            send(h, functools.partial(x_copy, h, i, n))
+        xbuf[chunk(direct[i]), slab(h, e), :] = xs[i, slab(h, e), :]
+
+    def x_arrived(h, i):
         for n in reversed(far_first):
-            s = (e + ne - n) % ne
-            where = pl.ds(at16(c * rows + s * half), half)
-            remote(xs.at[i, pl.ds(0, half)], xbuf.at[chunk(j), where], send.at[n], recv.at[n], {"expert": s}).wait_recv()
-
-    def y_copy(way, s, b, arriving=False):
+            t = (e + ne - n) % ne
+            remote(
+                xs.at[i, slab(h, 0)],
+                xbuf.at[chunk(direct[i]), slab(h, t)],
+                xs_sem.at[h, i, n],
+                xr_sem.at[h, i, n],
+                across(t, h),
+            ).wait_recv()
+
+    def y_copy(h, way, s, b, arriving=False):
         j = s + 1 if arriving else s
-        ref = xbuf.at[chunk(-j if way == 0 else j), pl.ds(at16(c * rows + b * sub), sub)]
-        return remote(ref, ref, ys_sem.at[way, s, b], yr_sem.at[way, s, b], right if way == 0 else left)
-
-    def share(j, b=0, n=parts, core=c):
-        i = j + hop
-        ref = xbuf.at[chunk(j), pl.ds(at16(core * rows + b * sub), n * sub)]
-        return remote(ref, ref, cs_sem.at[i, b], cr_sem.at[i, b], peer)
+        ref = xbuf.at[chunk(-j if way == 0 else j), pl.ds(h * rows + b * sub, sub)]
+        return remote(
+            ref, ref, ys_sem.at[h, way, s, b], yr_sem.at[h, way, s, b], chip(y + 1 if way == 0 else y - 1, h)
+        )
+
+    def share_copy(h, j):
+        ref = xbuf.at[chunk(j), pl.ds(h * rows, rows)]
+        return remote(ref, ref, cs_sem.at[h, j + hop], cr_sem.at[h, j + hop], peer)
+
+    def share(h, *chunks):
+        for j in chunks:
+            send(h, functools.partial(share_copy, h, j))
 
     def gemm(j, start=False):
         k = chunk(j)
-        if hop == abs(j):
-            for b in range(parts):
-                share(j, b, 1, 1 - c).wait_recv()
-        else:
-            share(j, core=1 - c).wait_recv()
+        for h in range(2):
+
+            @pl.when(jnp.logical_not(active[h]))
+            def _():
+                share_copy(h, j).wait_recv()
+
         lhs = xbuf[k]
         deep = pl.ds(pl.multiple_of(k * width, 128), width)
         for acc, w in ((acc_g, wg_v), (acc_u, wu_v)):
             term = jnp.dot(lhs, w[deep, :], preferred_element_type=F32)
             acc[...] = term if start else acc[...] + term
 
-    x_arrived(0, 0, xs_sem, xr_sem)
-    for b in range(parts):
-        for way in range(2):
-            go(y_copy(way, 0, b))
-    go(share(0))
-    for s in range(hop):
+    carry(lambda h: x_send(h, 0))
+    for i in range(1, len(direct)):
+        loads[2 + i].wait()
+        xs[i] = jnp.dot(picked, tok_v[i], preferred_element_type=F32).astype(BF16)
+        carry(lambda h: x_send(h, i))
+
+    def first_hop(h):
+        x_arrived(h, 0)
         for b in range(parts):
             for way in range(2):
-                y_copy(way, s, b, True).wait_recv()
-                if s + 1 < hop:
-                    go(y_copy(way, s + 1, b))
-                else:
-                    go(share(-hop if way == 0 else hop, b, 1))
-        if s + 1 < hop:
-            go(share(-1 - s))
-            go(share(s + 1))
-        if s == 0:
-            loads[4].wait()
-            loads[5].wait()
-            gemm(0, True)
-        if s == 1:
-            x_arrived(1, far, os_sem, or_sem)
-            go(share(far))
-        if s > 0:
-            gemm(-s)
-            gemm(s)
+                send(h, functools.partial(y_copy, h, way, 0, b))
+
+    def next_hop(s, h):
+        for b in range(parts):
+            for way in range(2):
+                y_copy(h, way, s, b, True).wait_recv()
+                if s + 1 < steps:
+                    send(h, functools.partial(y_copy, h, way, s + 1, b))
+
+    def x_rest(h, i):
+        x_arrived(h, i)
+        share(h, direct[i])
+
+    def last_hop(h):
+        next_hop(steps - 1, h)
+        share(h, -steps, steps)
+
+    carry(first_hop)
+
+    @pl.when(jnp.logical_not(jnp.logical_or(double, lone)))
+    def _():
+        for h in range(2):
+
+            @pl.when(active[h])
+            def _():
+                share_copy(h, 0).start()
+
+    for s in range(steps - 1):
+        carry(functools.partial(next_hop, s))
+
+    @pl.when(double)
+    def _():
+        pl.semaphore_wait(ready, 1)
+        share_copy(0, 0).start()
+        share_copy(1, 0).start()
+
+    for h in range(2):
+        sent_of[h].append(functools.partial(share_copy, h, 0))
+    carry(lambda h: share(h, *[j for k in range(1, steps) for j in (-k, k)]))
+    ahead = len(pairs) - 3
+    loads[ahead].wait()
+    loads[ahead + 1].wait()
+    gemm(0, True)
+    carry(lambda h: x_rest(h, 1))
+    for k in range(1, steps):
+        gemm(-k)
+        gemm(k)
+    carry(last_hop)
+    for i in range(2, len(direct)):
+        carry(lambda h: x_rest(h, i))
     gemm(far)
-    gemm(-hop)
-    gemm(hop)
+    for k in range(steps, far):
+        gemm(-k)
+        gemm(k)
+
+    @pl.when(beside)
+    def _():
+        pl.semaphore_wait(ready, 1)
 
     gate = acc_g[...]
     hid[...] = (gate / (1.0 + jnp.exp(-gate)) * acc_u[...]).astype(BF16)
-    loads[6].wait()
+    loads[ahead + 2].wait()
 
     low = lax.broadcasted_iota(jnp.int32, (rows, width), 1) < width // 2
 
@@ -313,6 +431,7 @@
     out[...] = total[:, : width // 2].astype(BF16)
     for copy in sent:
         copy.wait_send()
+    carry(lambda h: [make().wait_send() for make in sent_of[h]])
 
 
 def on_device(tokens, routes, route_weights, w_gate, w_up, w_down):
@@ -335,8 +454,8 @@
         scratch_shapes=[
             pltpu.VMEM((2, toks), jnp.int32),
             pltpu.VMEM((2, toks), F32),
-            pltpu.VMEM((2, toks, width), BF16),
-            pltpu.VMEM((2, rows, width), BF16),
+            pltpu.VMEM((4, toks, width), BF16),
+            pltpu.VMEM((4, 2 * rows, width), BF16),
             pltpu.VMEM((ny, 2 * rows, width), BF16),
             pltpu.VMEM((model, hidden), BF16),
             pltpu.VMEM((model, hidden), BF16),
@@ -351,21 +470,20 @@
             pltpu.VMEM((2, far, rows, width), BF16),
             pltpu.VMEM((rows, width), BF16),
             pltpu.VMEM((rows, width), BF16),
-            dma((7,)),
-            dma((ne,)),
-            dma((ne,)),
-            dma((ne,)),
-            dma((ne,)),
-            dma((2, far, 4)),
-            dma((2, far, 4)),
-            dma((ny, 4)),
-            dma((ny, 4)),
+            dma((9,)),
+            dma((2, 4, ne)),
+            dma((2, 4, ne)),
+            dma((2, 2, far - 2, 4)),
+            dma((2, 2, far - 2, 4)),
+            dma((2, ny)),
+            dma((2, ny)),
             dma((ny,)),
             dma((ny,)),
             dma((2, far, 4)),
             dma((2, far, 4)),
             dma((ne,)),
             dma((ne,)),
+            pltpu.SemaphoreType.REGULAR,
         ],
         compiler_params=pltpu.CompilerParams(
             collective_id=0, has_side_effects=True, vmem_limit_bytes=60 * 1024 * 1024

time: 58.2 us -> 51 us (0.88)
  the two profiles are of different devices: /device:TPU:2 before, /device:TPU:640 now
where the time goes in v3:
time: 51 us; the launch traced here: 50.8 us
  Pallas kernels  49.4 us (97%)
  local copies, waits for them, and re-layouts  1.42 us (3%)
    pallas_call x1, Pallas kernels, on_device(): pl.pallas_call(functools.partial(kernel, (ne, ny, half, width)), out_shap...  49.4 us
    unnamed x1, local copies, waits for them, and re-layouts  1.42 us

profile of v3, /device:TPU:640, one launch (start us, length us, event | category | flops | bytes accessed | tf_op | source)
XLA Modules:
  0.0 50.8 jit_solution(7267071660914951580)
XLA Ops:
  0.0 49.4 %shard_map.64 = bf16[96,192]{1,0:T(8,128)(2,1)} custom-call(bf16[96,3072]{1,0:T(8,128)(2,1)} %tokens.1, s32[2,96]{1,0:T(2,128)} %bitcast.2, f32[2,96]{1,0:T(2,128)} %bitcast.3, bf16[1,3072,512]{2,1,0:T(8,128)(2,1)} %wg.1, bf16[1,3072,512]{2,1,0:T(8,128)(2,1)} %wu.1, bf16[1,512,3072]{2,1,0:T(8,128)(2,1)} %wd.1), custom_call_target="tpu_custom_call" | custom-call | tf_op jit(solution)/shard_map/pallas_call | solution.py:449
  49.4 1.4 %copy.8 = bf16[96,192]{1,0:T(8,128)(2,1)} copy(bf16[96,192]{1,0:T(8,128)(2,1)} %shard_map.64) | data formatting | bytes 73728

commit v4 on v3

--- a/solution.py
+++ b/solution.py
@@ -36,6 +36,7 @@
     pk,
     cin,
     rin,
+    rin_o,
     rout,
     fin,
     rbuf,
@@ -52,6 +53,10 @@
     rr_sem,
     fs_sem,
     fr_sem,
+    ts_sem,
+    tr_sem,
+    os_sem,
+    or_sem,
     ready,
 ):
     ne, ny, half, width = dims
@@ -85,12 +90,12 @@
     right = {"pipe": (y + 1) % ny * 2 + c}
     left = {"pipe": (y + ny - 1) % ny * 2 + c}
     peer = {"pipe": 2 * y + 1 - c}
+    slant = [{"pipe": (y + 1) % ny * 2 + 1 - c}, {"pipe": (y + ny - 1) % ny * 2 + 1 - c}]
     front = d == 0
     lone = jnp.logical_and(front, jnp.logical_and(pipe == 0, e == 0))
     double = jnp.logical_and(front, jnp.logical_and(pipe == 1, e == 0))
-    in_row = jnp.logical_and(y == 0, e != 0)
-    in_column = jnp.logical_and(e == 0, jnp.logical_or(y == 1, y == ny - 1))
-    beside = jnp.logical_and(jnp.logical_and(front, c == 0), jnp.logical_or(in_row, in_column))
+    in_row = jnp.logical_and(jnp.logical_and(front, pipe == 0), e != 0)
+    column = jnp.logical_and(jnp.logical_and(front, e == 0), jnp.logical_or(y == 1, y == ny - 1))
     active = [carrier(y, e, h) == c for h in range(2)]
 
     def chunk(j):
@@ -127,7 +132,7 @@
     def greet(semaphore, device):
         pl.semaphore_signal(semaphore, inc=1, device_id=device, device_id_type=MESH)
 
-    neighbours = [{"expert": (e + j) % ne} for j in range(1, ne)] + [right, left, peer]
+    neighbours = [{"expert": (e + j) % ne} for j in range(1, ne)] + [right, left, peer, *slant]
 
     @pl.when(jnp.logical_not(lone))
     def _():
@@ -136,10 +141,10 @@
 
     @pl.when(double)
     def _():
-        for device in [{"pipe": 0, "expert": t} for t in range(1, ne)] + [{"pipe": 2}, {"pipe": 2 * ny - 2}]:
-            greet(barrier, device)
-
-    @pl.when(beside)
+        for t in range(1, ne):
+            greet(barrier, {"pipe": 0, "expert": t})
+
+    @pl.when(in_row)
     def _():
         greet(barrier, {"pipe": 1, "expert": 0})
 
@@ -174,13 +179,17 @@
     loads[2].wait()
     xs[0] = jnp.dot(picked, tok_v[0], preferred_element_type=F32).astype(BF16)
 
-    @pl.when(jnp.logical_not(double))
+    @pl.when(jnp.logical_not(jnp.logical_or(double, column)))
     def _():
         pl.semaphore_wait(barrier, len(neighbours))
 
+    @pl.when(column)
+    def _():
+        pl.semaphore_wait(barrier, len(neighbours) - 1)
+
     @pl.when(double)
     def _():
-        pl.semaphore_wait(barrier, 2 * len(neighbours) - 2)
+        pl.semaphore_wait(barrier, len(neighbours) + ne - 2)
 
     @pl.when(lone)
     def _():
@@ -225,6 +234,16 @@
             ref, ref, ys_sem.at[h, way, s, b], yr_sem.at[h, way, s, b], chip(y + 1 if way == 0 else y - 1, h)
         )
 
+    to_open = [
+        jnp.logical_not(jnp.logical_and(jnp.logical_and(front, e == 0), (y + step + ny) % ny == 0)) for step in (1, -1)
+    ]
+
+    def twin_copy(h, way, b, arriving=False):
+        j = steps if arriving else steps - 1
+        ref = xbuf.at[chunk(-j if way == 0 else j), pl.ds(h * rows + b * sub, sub)]
+        at_y = (y + (1 if way == 0 else -1) + ny) % ny
+        return remote(ref, ref, ts_sem.at[h, way, b], tr_sem.at[h, way, b], {"pipe": 2 * at_y + 1 - h})
+
     def share_copy(h, j):
         ref = xbuf.at[chunk(j), pl.ds(h * rows, rows)]
         return remote(ref, ref, cs_sem.at[h, j + hop], cr_sem.at[h, j + hop], peer)
@@ -237,9 +256,22 @@
         k = chunk(j)
         for h in range(2):
 
-            @pl.when(jnp.logical_not(active[h]))
-            def _():
-                share_copy(h, j).wait_recv()
+            if abs(j) == steps:
+
+                @pl.when(jnp.logical_not(jnp.logical_or(active[h], lone)))
+                def _():
+                    for b in range(parts):
+                        twin_copy(h, 0 if j < 0 else 1, b, True).wait_recv()
+
+                @pl.when(lone)
+                def _():
+                    share_copy(h, j).wait_recv()
+
+            else:
+
+                @pl.when(jnp.logical_not(active[h]))
+                def _():
+                    share_copy(h, j).wait_recv()
 
         lhs = xbuf[k]
         deep = pl.ds(pl.multiple_of(k * width, 128), width)
@@ -265,6 +297,11 @@
                 y_copy(h, way, s, b, True).wait_recv()
                 if s + 1 < steps:
                     send(h, functools.partial(y_copy, h, way, s + 1, b))
+                if s + 2 == steps:
+
+                    @pl.when(to_open[way])
+                    def _():
+                        twin_copy(h, way, b).start()
 
     def x_rest(h, i):
         x_arrived(h, i)
@@ -272,7 +309,11 @@
 
     def last_hop(h):
         next_hop(steps - 1, h)
-        share(h, -steps, steps)
+
+        @pl.when(double)
+        def _():
+            share_copy(h, -steps).start()
+            share_copy(h, steps).start()
 
     carry(first_hop)
 
@@ -312,7 +353,7 @@
         gemm(-k)
         gemm(k)
 
-    @pl.when(beside)
+    @pl.when(jnp.logical_or(in_row, column))
     def _():
         pl.semaphore_wait(ready, 1)
 
@@ -329,7 +370,8 @@
         a, b = part[:rows], part[rows:]
         pk[i, 0] = jnp.where(low, a, pltpu.roll(b, width // 2, 1)).astype(BF16)
         pk[i, 1] = jnp.where(low, pltpu.roll(a, width // 2, 1), b).astype(BF16)
-        go(remote(pk.at[i, 1 - c], cin.at[i], ds_sem.at[i], dr_sem.at[i], peer))
+        if j != far:
+            go(remote(pk.at[i, 1 - c], cin.at[i], ds_sem.at[i], dr_sem.at[i], peer))
 
     def met(j):
         i = j + hop
@@ -354,25 +396,42 @@
         r_copy(way, s, b).wait_recv()
         return rin[way, s, pl.ds(b * sub, sub), :].astype(F32)
 
+    def first_copy(way, b, other):
+        at = pl.ds(b * sub, sub)
+        if other:
+            return remote(
+                pk.at[far + hop, 1 - c, at], rin_o.at[way, at], os_sem.at[way, b], or_sem.at[way, b], slant[way]
+            )
+        return remote(
+            pk.at[far + hop, c, at],
+            rin.at[way, 0, at],
+            rs_sem.at[way, 0, b],
+            rr_sem.at[way, 0, b],
+            right if way == 0 else left,
+        )
+
+    def got_first(way, b):
+        first_copy(way, b, True).wait_recv()
+        return got(way, 0, b) + rin_o[way, pl.ds(b * sub, sub), :].astype(F32)
+
     def pass_on(way, s, b):
-        if s == 0:
-            total = own(far, b)
-        else:
-            total = own(far - s if way == 0 else s - far, b)
-            if s > 1 or b // (parts // 2) == way:
-                total = total + got(way, s - 1, b)
+        total = own(far - s if way == 0 else s - far, b)
+        if s > 1:
+            total = total + got(way, s - 1, b)
+        elif b // (parts // 2) == way:
+            total = total + got_first(way, b)
         rout[way, s, pl.ds(b * sub, sub), :] = total.astype(BF16)
         go(r_copy(way, s, b))
 
     down(far)
+    early, late = range(parts // 2), range(parts // 2, parts)
+    for b in early:
+        for other in (True, False):
+            go(first_copy(0, b, other))
+            go(first_copy(1, parts - 1 - b, other))
     for j in range(far - 1, max(0, far - 3), -1):
         down(j)
         down(-j)
-    early, late = range(parts // 2), range(parts // 2, parts)
-    met(far)
-    for b in early:
-        pass_on(0, 0, b)
-        pass_on(1, 0, parts - 1 - b)
     met(far - 1)
     met(1 - far)
     for b in late:
@@ -431,7 +490,23 @@
     out[...] = total[:, : width // 2].astype(BF16)
     for copy in sent:
         copy.wait_send()
-    carry(lambda h: [make().wait_send() for make in sent_of[h]])
+
+    def sent_all(h):
+        for make in sent_of[h]:
+            make().wait_send()
+        for way in range(2):
+
+            @pl.when(to_open[way])
+            def _():
+                for b in range(parts):
+                    twin_copy(h, way, b).wait_send()
+
+        @pl.when(double)
+        def _():
+            share_copy(h, -steps).wait_send()
+            share_copy(h, steps).wait_send()
+
+    carry(sent_all)
 
 
 def on_device(tokens, routes, route_weights, w_gate, w_up, w_down):
@@ -467,6 +542,7 @@
             pltpu.VMEM((ny, 2, rows, width), BF16),
             pltpu.VMEM((ny, rows, width), BF16),
             pltpu.VMEM((2, far, rows, width), BF16),
+            pltpu.VMEM((2, rows, width), BF16),
             pltpu.VMEM((2, far, rows, width), BF16),
             pltpu.VMEM((rows, width), BF16),
             pltpu.VMEM((rows, width), BF16),
@@ -483,6 +559,10 @@
             dma((2, far, 4)),
             dma((ne,)),
             dma((ne,)),
+            dma((2, 2, 4)),
+            dma((2, 2, 4)),
+            dma((2, 4)),
+            dma((2, 4)),
             pltpu.SemaphoreType.REGULAR,
         ],
         compiler_params=pltpu.CompilerParams(

time: 51 us -> 50.9 us (level)
  no operation moved by 1% of the time
where the time goes in v4:
time: 50.9 us; the launch traced here: 50.7 us
  Pallas kernels  49.3 us (97%)
  local copies, waits for them, and re-layouts  1.42 us (3%)
    pallas_call x1, Pallas kernels, on_device(): pl.pallas_call(functools.partial(kernel, (ne, ny, half, width)), out_shap...  49.3 us
    unnamed x1, local copies, waits for them, and re-layouts  1.42 us

profile of v4, /device:TPU:640, one launch (start us, length us, event | category | flops | bytes accessed | tf_op | source)
XLA Modules:
  0.0 50.7 jit_solution(14194372132839546835)
XLA Ops:
  0.0 49.3 %shard_map.64 = bf16[96,192]{1,0:T(8,128)(2,1)} custom-call(bf16[96,3072]{1,0:T(8,128)(2,1)} %tokens.1, s32[2,96]{1,0:T(2,128)} %bitcast.2, f32[2,96]{1,0:T(2,128)} %bitcast.3, bf16[1,3072,512]{2,1,0:T(8,128)(2,1)} %wg.1, bf16[1,3072,512]{2,1,0:T(8,128)(2,1)} %wu.1, bf16[1,512,3072]{2,1,0:T(8,128)(2,1)} %wd.1), custom_call_target="tpu_custom_call" | custom-call | tf_op jit(solution)/shard_map/pallas_call | solution.py:524
  49.3 1.4 %copy.8 = bf16[96,192]{1,0:T(8,128)(2,1)} copy(bf16[96,192]{1,0:T(8,128)(2,1)} %shard_map.64) | data formatting | bytes 73728

commit v5 on v3

--- a/solution.py
+++ b/solution.py
@@ -122,27 +122,6 @@
             def _():
                 work(h)
 
-    barrier = pltpu.get_barrier_semaphore()
-
-    def greet(semaphore, device):
-        pl.semaphore_signal(semaphore, inc=1, device_id=device, device_id_type=MESH)
-
-    neighbours = [{"expert": (e + j) % ne} for j in range(1, ne)] + [right, left, peer]
-
-    @pl.when(jnp.logical_not(lone))
-    def _():
-        for device in neighbours:
-            greet(barrier, device)
-
-    @pl.when(double)
-    def _():
-        for device in [{"pipe": 0, "expert": t} for t in range(1, ne)] + [{"pipe": 2}, {"pipe": 2 * ny - 2}]:
-            greet(barrier, device)
-
-    @pl.when(beside)
-    def _():
-        greet(barrier, {"pipe": 1, "expert": 0})
-
     pairs = [(routes, route_v), (route_w, weight_v)]
     direct = [0, far] + [j for k in range(steps + 1, far) for j in (-k, k)]
     for i, j in enumerate(direct):
@@ -152,6 +131,27 @@
     loads = [pltpu.make_async_copy(src, dst, load_sem.at[i]) for i, (src, dst) in enumerate(pairs)]
     for copy in loads:
         copy.start()
+
+    barrier = pltpu.get_barrier_semaphore()
+
+    def greet(semaphore, device):
+        pl.semaphore_signal(semaphore, inc=1, device_id=device, device_id_type=MESH)
+
+    neighbours = [{"expert": (e + j) % ne} for j in range(1, ne)] + [right, left, peer]
+
+    @pl.when(jnp.logical_not(lone))
+    def _():
+        for device in neighbours:
+            greet(barrier, device)
+
+    @pl.when(double)
+    def _():
+        for device in [{"pipe": 0, "expert": t} for t in range(1, ne)] + [{"pipe": 2}, {"pipe": 2 * ny - 2}]:
+            greet(barrier, device)
+
+    @pl.when(beside)
+    def _():
+        greet(barrier, {"pipe": 1, "expert": 0})
 
     toks = tok_v.shape[1]
     row = lax.broadcasted_iota(jnp.int32, (2 * rows, toks), 0)
@@ -304,13 +304,13 @@
     for k in range(1, steps):
         gemm(-k)
         gemm(k)
+    carry(lambda h: x_rest(h, 2))
+    gemm(far)
     carry(last_hop)
-    for i in range(2, len(direct)):
+    for i in range(3, len(direct)):
         carry(lambda h: x_rest(h, i))
-    gemm(far)
-    for k in range(steps, far):
-        gemm(-k)
-        gemm(k)
+    for j in (direct[2], -steps, steps, *direct[3:]):
+        gemm(j)
 
     @pl.when(beside)
     def _():
@@ -415,6 +415,9 @@
     weights = mix[...].T
     hi = weights.astype(BF16)
     lo = (weights - hi.astype(F32)).astype(BF16)
+    for copy in sent:
+        copy.wait_send()
+    carry(lambda h: [make().wait_send() for make in sent_of[h]])
     for n in range(1, ne):
         t = (e + n) % ne
         at = pl.ds(at16(t * half), half)
@@ -429,9 +432,6 @@
 
     total = mixed(0) + pltpu.roll(mixed(1), width // 2, 1)
     out[...] = total[:, : width // 2].astype(BF16)
-    for copy in sent:
-        copy.wait_send()
-    carry(lambda h: [make().wait_send() for make in sent_of[h]])
 
 
 def on_device(tokens, routes, route_weights, w_gate, w_up, w_down):
@@ -486,7 +486,7 @@
             pltpu.SemaphoreType.REGULAR,
         ],
         compiler_params=pltpu.CompilerParams(
-            collective_id=0, has_side_effects=True, vmem_limit_bytes=60 * 1024 * 1024
+            collective_id=0, has_side_effects=True, vmem_limit_bytes=54784 * 1024
         ),
     )(tokens, routes.T, route_weights.T, w_gate, w_up, w_down)
 

time: 51 us -> 50.5 us (level)
  the two profiles are of different devices: /device:TPU:640 before, /device:TPU:768 now
where the time goes in v5:
time: 50.5 us; the launch traced here: 50.3 us
  Pallas kernels  48.3 us (96%)
  local copies, waits for them, and re-layouts  1.98 us (4%)
    pallas_call x1, Pallas kernels, on_device(): pl.pallas_call(functools.partial(kernel, (ne, ny, half, width)), out_shap...  48.3 us
    unnamed x5, local copies, waits for them, and re-layouts  1.98 us

profile of v5, /device:TPU:768, one launch (start us, length us, event | category | flops | bytes accessed | tf_op | source)
XLA Modules:
  0.0 50.3 jit_solution(4265790149272033508)
XLA Ops:
  0.0 0.0 copy-start
  0.0 0.7 %copy-done = s32[96,2]{0,1:T(2,128)S(1)} copy-done((s32[96,2]{0,1:T(2,128)S(1)}, s32[96,2]{0,1:T(2,128)}, u32[]{:S(2)}) %copy-start) | copy-done | bytes 792
  0.7 0.0 copy-start.1
  0.7 0.7 %copy-done.1 = f32[96,2]{0,1:T(2,128)S(1)} copy-done((f32[96,2]{0,1:T(2,128)S(1)}, f32[96,2]{0,1:T(2,128)}, u32[]{:S(2)}) %copy-start.1) | copy-done | bytes 792
  1.4 48.3 %shard_map.64 = bf16[96,192]{1,0:T(8,128)(2,1)S(1)} custom-call(bf16[96,3072]{1,0:T(8,128)(2,1)} %tokens.1, s32[2,96]{1,0:T(2,128)S(1)} %bitcast.2, f32[2,96]{1,0:T(2,128)S(1)} %bitcast.3, bf16[1,3072,512]{2,1,0:T(8,128)(2,1)} %wg.1, bf16[1,3072,512]{2,1,0:T(8,128)(2,1)} %wu.1, bf16[1,512,3072]{2,1,0:T(8,128)(2,1)} %wd.1), custom_call_target="tpu_custom_call" | custom-call | tf_op jit(solution)/shard_map/pallas_call | solution.py:449
  49.7 0.6 %copy.8 = bf16[96,192]{1,0:T(8,128)(2,1)} copy(bf16[96,192]{1,0:T(8,128)(2,1)S(1)} %shard_map.64) | data formatting | bytes 73728
Async XLA Ops:
  0.0 0.7 %copy-start = (s32[96,2]{0,1:T(2,128)S(1)}, s32[96,2]{0,1:T(2,128)}, u32[]{:S(2)}) copy-start(s32[96,2]{0,1:T(2,128)} %param.7) | copy-start | bytes 2308
  0.7 0.7 %copy-start.1 = (f32[96,2]{0,1:T(2,128)S(1)}, f32[96,2]{0,1:T(2,128)}, u32[]{:S(2)}) copy-start(f32[96,2]{0,1:T(2,128)} %param.8) | copy-start | bytes 2308

commit v6 on v5

--- a/solution.py
+++ b/solution.py
@@ -58,6 +58,7 @@
     rows = ne * half
     parts = 4
     sub = rows // parts
+    per = ne // parts
     pipe = lax.axis_index("pipe")
     e = lax.axis_index("expert")
     y = pipe // 2
@@ -95,6 +96,17 @@
 
     def chunk(j):
         return (y + j + ny) % ny
+
+    base = e // per
+    near_first, far_first_parts = (0, 1, 3, 2), (2, 1, 3, 0)
+
+    def part(k):
+        return pl.multiple_of((base + k) % parts * sub, sub)
+
+    def others(k):
+        if k:
+            return [(base + k) % parts * per + m for m in range(per)]
+        return [base * per + (e + m) % per for m in range(1, per)]
 
     def at16(x):
         return pl.multiple_of(x, 16)
@@ -220,7 +232,7 @@
 
     def y_copy(h, way, s, b, arriving=False):
         j = s + 1 if arriving else s
-        ref = xbuf.at[chunk(-j if way == 0 else j), pl.ds(h * rows + b * sub, sub)]
+        ref = xbuf.at[chunk(-j if way == 0 else j), pl.ds(pl.multiple_of(h * rows + part(b), sub), sub)]
         return remote(
             ref, ref, ys_sem.at[h, way, s, b], yr_sem.at[h, way, s, b], chip(y + 1 if way == 0 else y - 1, h)
         )
@@ -254,13 +266,21 @@
         carry(lambda h: x_send(h, i))
 
     def first_hop(h):
-        x_arrived(h, 0)
-        for b in range(parts):
+        for b in near_first:
+            for t in others(b):
+                n = (e + ne - t) % ne
+                remote(
+                    xs.at[0, slab(h, 0)],
+                    xbuf.at[chunk(0), slab(h, t)],
+                    xs_sem.at[h, 0, n],
+                    xr_sem.at[h, 0, n],
+                    across(t, h),
+                ).wait_recv()
             for way in range(2):
                 send(h, functools.partial(y_copy, h, way, 0, b))
 
     def next_hop(s, h):
-        for b in range(parts):
+        for b in near_first:
             for way in range(2):
                 y_copy(h, way, s, b, True).wait_recv()
                 if s + 1 < steps:
@@ -337,11 +357,11 @@
 
     def own(j, b):
         i = j + hop
-        at = pl.ds(b * sub, sub)
+        at = pl.ds(part(b), sub)
         return pk[i, c, at, :].astype(F32) + cin[i, at, :].astype(F32)
 
     def r_copy(way, s, b):
-        at = pl.ds(b * sub, sub)
+        at = pl.ds(part(b), sub)
         return remote(
             rout.at[way, s, at],
             rin.at[way, s, at],
@@ -352,7 +372,7 @@
 
     def got(way, s, b):
         r_copy(way, s, b).wait_recv()
-        return rin[way, s, pl.ds(b * sub, sub), :].astype(F32)
+        return rin[way, s, pl.ds(part(b), sub), :].astype(F32)
 
     def pass_on(way, s, b):
         if s == 0:
@@ -361,14 +381,14 @@
             total = own(far - s if way == 0 else s - far, b)
             if s > 1 or b // (parts // 2) == way:
                 total = total + got(way, s - 1, b)
-        rout[way, s, pl.ds(b * sub, sub), :] = total.astype(BF16)
+        rout[way, s, pl.ds(part(b), sub), :] = total.astype(BF16)
         go(r_copy(way, s, b))
 
     down(far)
     for j in range(far - 1, max(0, far - 3), -1):
         down(j)
         down(-j)
-    early, late = range(parts // 2), range(parts // 2, parts)
+    early, late = (1, 0), (2, 3)
     met(far)
     for b in early:
         pass_on(0, 0, b)
@@ -388,28 +408,23 @@
     for s in range(2, far):
         met(far - s)
         met(s - far)
-        for b in (*late, *early):
+        for b in far_first_parts:
             pass_on(0, s, b)
-            pass_on(1, s, parts - 1 - b)
+            pass_on(1, s, b)
     met(0)
 
-    per = ne // parts
     own_back = pl.ds(at16(e * half), half)
 
     def back_copy(t):
         return remote(
-            fin.at[pl.ds(t * half, half)], rbuf.at[own_back], fs_sem.at[t], fr_sem.at[e], {"expert": t}
+            fin.at[pl.ds(at16(t * half), half)], rbuf.at[own_back], fs_sem.at[t], fr_sem.at[e], {"expert": t}
         )
 
-    order = [b for pair in zip(late, reversed(early)) for b in pair]
-    for b in order:
+    for b in far_first_parts:
         total = own(0, b) + got(0, far - 1, b) + got(1, far - 1, b)
-        fin[pl.ds(b * sub, sub), :] = total.astype(BF16)
-        for t in range(b * per, b * per + per):
-
-            @pl.when(t != e)
-            def _():
-                back_copy(t).start()
+        fin[pl.ds(part(b), sub), :] = total.astype(BF16)
+        for t in others(b):
+            back_copy(t).start()
 
     rbuf[own_back, :] = fin[own_back, :]
     weights = mix[...].T

time: 50.5 us -> 49.1 us (0.972)
  the two profiles are of different devices: /device:TPU:768 before, /device:TPU:770 now
where the time goes in v6:
time: 49.1 us; the launch traced here: 48.9 us
  Pallas kernels  47 us (96%)
  local copies, waits for them, and re-layouts  1.98 us (4%)
    pallas_call x1, Pallas kernels, on_device(): pl.pallas_call(functools.partial(kernel, (ne, ny, half, width)), out_shap...  47 us
    unnamed x5, local copies, waits for them, and re-layouts  1.98 us

profile of v6, /device:TPU:770, one launch (start us, length us, event | category | flops | bytes accessed | tf_op | source)
XLA Modules:
  0.0 48.9 jit_solution(3814997854332465947)
XLA Ops:
  0.0 0.0 copy-start
  0.0 0.7 %copy-done = s32[96,2]{0,1:T(2,128)S(1)} copy-done((s32[96,2]{0,1:T(2,128)S(1)}, s32[96,2]{0,1:T(2,128)}, u32[]{:S(2)}) %copy-start) | copy-done | bytes 792
  0.7 0.0 copy-start.1
  0.7 0.7 %copy-done.1 = f32[96,2]{0,1:T(2,128)S(1)} copy-done((f32[96,2]{0,1:T(2,128)S(1)}, f32[96,2]{0,1:T(2,128)}, u32[]{:S(2)}) %copy-start.1) | copy-done | bytes 792
  1.4 47.0 %shard_map.64 = bf16[96,192]{1,0:T(8,128)(2,1)S(1)} custom-call(bf16[96,3072]{1,0:T(8,128)(2,1)} %tokens.1, s32[2,96]{1,0:T(2,128)S(1)} %bitcast.2, f32[2,96]{1,0:T(2,128)S(1)} %bitcast.3, bf16[1,3072,512]{2,1,0:T(8,128)(2,1)} %wg.1, bf16[1,3072,512]{2,1,0:T(8,128)(2,1)} %wu.1, bf16[1,512,3072]{2,1,0:T(8,128)(2,1)} %wd.1), custom_call_target="tpu_custom_call" | custom-call | tf_op jit(solution)/shard_map/pallas_call | solution.py:464
  48.3 0.6 %copy.8 = bf16[96,192]{1,0:T(8,128)(2,1)} copy(bf16[96,192]{1,0:T(8,128)(2,1)S(1)} %shard_map.64) | data formatting | bytes 73728
Async XLA Ops:
  0.0 0.7 %copy-start = (s32[96,2]{0,1:T(2,128)S(1)}, s32[96,2]{0,1:T(2,128)}, u32[]{:S(2)}) copy-start(s32[96,2]{0,1:T(2,128)} %param.7) | copy-start | bytes 2308
  0.7 0.7 %copy-start.1 = (f32[96,2]{0,1:T(2,128)S(1)}, f32[96,2]{0,1:T(2,128)}, u32[]{:S(2)}) copy-start(f32[96,2]{0,1:T(2,128)} %param.8) | copy-start | bytes 2308

commit v7 on v6

--- a/solution.py
+++ b/solution.py
@@ -86,11 +86,14 @@
     right = {"pipe": (y + 1) % ny * 2 + c}
     left = {"pipe": (y + ny - 1) % ny * 2 + c}
     peer = {"pipe": 2 * y + 1 - c}
+    two_on = [{"pipe": (y + 2) % ny * 2 + c}, {"pipe": (y + ny - 2) % ny * 2 + c}]
     front = d == 0
     lone = jnp.logical_and(front, jnp.logical_and(pipe == 0, e == 0))
     double = jnp.logical_and(front, jnp.logical_and(pipe == 1, e == 0))
     in_row = jnp.logical_and(y == 0, e != 0)
     in_column = jnp.logical_and(e == 0, jnp.logical_or(y == 1, y == ny - 1))
+    in_second = jnp.logical_and(e == 0, jnp.logical_or(y == 2, y == ny - 2))
+    second_on = jnp.logical_and(jnp.logical_and(front, c == 0), in_second)
     beside = jnp.logical_and(jnp.logical_and(front, c == 0), jnp.logical_or(in_row, in_column))
     active = [carrier(y, e, h) == c for h in range(2)]
 
@@ -149,7 +152,7 @@
     def greet(semaphore, device):
         pl.semaphore_signal(semaphore, inc=1, device_id=device, device_id_type=MESH)
 
-    neighbours = [{"expert": (e + j) % ne} for j in range(1, ne)] + [right, left, peer]
+    neighbours = [{"expert": (e + j) % ne} for j in range(1, ne)] + [right, left, peer, *two_on]
 
     @pl.when(jnp.logical_not(lone))
     def _():
@@ -186,13 +189,17 @@
     loads[2].wait()
     xs[0] = jnp.dot(picked, tok_v[0], preferred_element_type=F32).astype(BF16)
 
-    @pl.when(jnp.logical_not(double))
+    @pl.when(jnp.logical_not(jnp.logical_or(double, second_on)))
     def _():
         pl.semaphore_wait(barrier, len(neighbours))
 
+    @pl.when(second_on)
+    def _():
+        pl.semaphore_wait(barrier, len(neighbours) - 1)
+
     @pl.when(double)
     def _():
-        pl.semaphore_wait(barrier, 2 * len(neighbours) - 2)
+        pl.semaphore_wait(barrier, len(neighbours) - 1 + ne - 1 + 2)
 
     @pl.when(lone)
     def _():
@@ -332,7 +339,7 @@
     for j in (direct[2], -steps, steps, *direct[3:]):
         gemm(j)
 
-    @pl.when(beside)
+    @pl.when(jnp.logical_or(beside, second_on))
     def _():
         pl.semaphore_wait(ready, 1)
 
@@ -367,7 +374,7 @@
             rin.at[way, s, at],
             rs_sem.at[way, s, b],
             rr_sem.at[way, s, b],
-            right if way == 0 else left,
+            two_on[way] if s == 0 else right if way == 0 else left,
         )
 
     def got(way, s, b):
@@ -375,12 +382,11 @@
         return rin[way, s, pl.ds(part(b), sub), :].astype(F32)
 
     def pass_on(way, s, b):
-        if s == 0:
-            total = own(far, b)
-        else:
-            total = own(far - s if way == 0 else s - far, b)
-            if s > 1 or b // (parts // 2) == way:
-                total = total + got(way, s - 1, b)
+        total = own(far - s if s == 0 or way == 0 else s - far, b)
+        if s > 1:
+            total = total + got(way, s - 1, b)
+        if s == 2 and b // (parts // 2) == way:
+            total = total + got(way, 0, b)
         rout[way, s, pl.ds(part(b), sub), :] = total.astype(BF16)
         go(r_copy(way, s, b))
 
@@ -388,23 +394,20 @@
     for j in range(far - 1, max(0, far - 3), -1):
         down(j)
         down(-j)
-    early, late = (1, 0), (2, 3)
+    early = (1, 0)
     met(far)
     for b in early:
         pass_on(0, 0, b)
         pass_on(1, 0, parts - 1 - b)
     met(far - 1)
     met(1 - far)
-    for b in late:
+    for b in far_first_parts:
         pass_on(0, 1, b)
-        pass_on(1, 1, parts - 1 - b)
+        pass_on(1, 1, b)
     for j in range(far - 3, 0, -1):
         down(j)
         down(-j)
     down(0)
-    for b in early:
-        pass_on(0, 1, b)
-        pass_on(1, 1, parts - 1 - b)
     for s in range(2, far):
         met(far - s)
         met(s - far)

time: 49.1 us -> 48.5 us (0.988)
  Pallas kernels: 47 us -> 46.3 us
    pallas_call x1, Pallas kernels: 47 us -> 46.3 us  [on_device(): pl.pallas_call(functools.partial(kernel, (ne, ny, half, width)), out_shap...]
where the time goes in v7:
time: 48.5 us; the launch traced here: 48.3 us
  Pallas kernels  46.3 us (95%)
  local copies, waits for them, and re-layouts  1.98 us (4%)
    pallas_call x1, Pallas kernels, on_device(): pl.pallas_call(functools.partial(kernel, (ne, ny, half, width)), out_shap...  46.3 us
    unnamed x5, local copies, waits for them, and re-layouts  1.98 us

profile of v7, /device:TPU:770, one launch (start us, length us, event | category | flops | bytes accessed | tf_op | source)
XLA Modules:
  0.0 48.3 jit_solution(2697783998311681802)
XLA Ops:
  0.0 0.0 copy-start
  0.0 0.7 %copy-done = s32[96,2]{0,1:T(2,128)S(1)} copy-done((s32[96,2]{0,1:T(2,128)S(1)}, s32[96,2]{0,1:T(2,128)}, u32[]{:S(2)}) %copy-start) | copy-done | bytes 792
  0.7 0.0 copy-start.1
  0.7 0.7 %copy-done.1 = f32[96,2]{0,1:T(2,128)S(1)} copy-done((f32[96,2]{0,1:T(2,128)S(1)}, f32[96,2]{0,1:T(2,128)}, u32[]{:S(2)}) %copy-start.1) | copy-done | bytes 792
  1.4 46.3 %shard_map.64 = bf16[96,192]{1,0:T(8,128)(2,1)S(1)} custom-call(bf16[96,3072]{1,0:T(8,128)(2,1)} %tokens.1, s32[2,96]{1,0:T(2,128)S(1)} %bitcast.2, f32[2,96]{1,0:T(2,128)S(1)} %bitcast.3, bf16[1,3072,512]{2,1,0:T(8,128)(2,1)} %wg.1, bf16[1,3072,512]{2,1,0:T(8,128)(2,1)} %wu.1, bf16[1,512,3072]{2,1,0:T(8,128)(2,1)} %wd.1), custom_call_target="tpu_custom_call" | custom-call | tf_op jit(solution)/shard_map/pallas_call | solution.py:467
  47.7 0.6 %copy.8 = bf16[96,192]{1,0:T(8,128)(2,1)} copy(bf16[96,192]{1,0:T(8,128)(2,1)S(1)} %shard_map.64) | data formatting | bytes 73728
Async XLA Ops:
  0.0 0.7 %copy-start = (s32[96,2]{0,1:T(2,128)S(1)}, s32[96,2]{0,1:T(2,128)}, u32[]{:S(2)}) copy-start(s32[96,2]{0,1:T(2,128)} %param.7) | copy-start | bytes 2308
  0.7 0.7 %copy-start.1 = (f32[96,2]{0,1:T(2,128)S(1)}, f32[96,2]{0,1:T(2,128)}, u32[]{:S(2)}) copy-start(f32[96,2]{0,1:T(2,128)} %param.8) | copy-start | bytes 2308

commit v8 on v7

--- a/solution.py
+++ b/solution.py
@@ -391,7 +391,7 @@
         go(r_copy(way, s, b))
 
     down(far)
-    for j in range(far - 1, max(0, far - 3), -1):
+    for j in (far - 1,):
         down(j)
         down(-j)
     early = (1, 0)
@@ -404,7 +404,7 @@
     for b in far_first_parts:
         pass_on(0, 1, b)
         pass_on(1, 1, b)
-    for j in range(far - 3, 0, -1):
+    for j in range(far - 2, 0, -1):
         down(j)
         down(-j)
     down(0)

time: 48.5 us -> 48 us (0.990)
  no operation moved by 1% of the time
where the time goes in v8:
time: 48 us; the launch traced here: 47.9 us
  Pallas kernels  45.9 us (96%)
  local copies, waits for them, and re-layouts  1.98 us (4%)
    pallas_call x1, Pallas kernels, on_device(): pl.pallas_call(functools.partial(kernel, (ne, ny, half, width)), out_shap...  45.9 us
    unnamed x5, local copies, waits for them, and re-layouts  1.98 us

profile of v8, /device:TPU:770, one launch (start us, length us, event | category | flops | bytes accessed | tf_op | source)
XLA Modules:
  0.0 47.9 jit_solution(9372034414674683864)
XLA Ops:
  0.0 0.0 copy-start
  0.0 0.7 %copy-done = s32[96,2]{0,1:T(2,128)S(1)} copy-done((s32[96,2]{0,1:T(2,128)S(1)}, s32[96,2]{0,1:T(2,128)}, u32[]{:S(2)}) %copy-start) | copy-done | bytes 792
  0.7 0.0 copy-start.1
  0.7 0.7 %copy-done.1 = f32[96,2]{0,1:T(2,128)S(1)} copy-done((f32[96,2]{0,1:T(2,128)S(1)}, f32[96,2]{0,1:T(2,128)}, u32[]{:S(2)}) %copy-start.1) | copy-done | bytes 792
  1.4 45.9 %shard_map.64 = bf16[96,192]{1,0:T(8,128)(2,1)S(1)} custom-call(bf16[96,3072]{1,0:T(8,128)(2,1)} %tokens.1, s32[2,96]{1,0:T(2,128)S(1)} %bitcast.2, f32[2,96]{1,0:T(2,128)S(1)} %bitcast.3, bf16[1,3072,512]{2,1,0:T(8,128)(2,1)} %wg.1, bf16[1,3072,512]{2,1,0:T(8,128)(2,1)} %wu.1, bf16[1,512,3072]{2,1,0:T(8,128)(2,1)} %wd.1), custom_call_target="tpu_custom_call" | custom-call | tf_op jit(solution)/shard_map/pallas_call | solution.py:467
  47.2 0.6 %copy.8 = bf16[96,192]{1,0:T(8,128)(2,1)} copy(bf16[96,192]{1,0:T(8,128)(2,1)S(1)} %shard_map.64) | data formatting | bytes 73728
Async XLA Ops:
  0.0 0.7 %copy-start = (s32[96,2]{0,1:T(2,128)S(1)}, s32[96,2]{0,1:T(2,128)}, u32[]{:S(2)}) copy-start(s32[96,2]{0,1:T(2,128)} %param.7) | copy-start | bytes 2308
  0.7 0.7 %copy-start.1 = (f32[96,2]{0,1:T(2,128)S(1)}, f32[96,2]{0,1:T(2,128)}, u32[]{:S(2)}) copy-start(f32[96,2]{0,1:T(2,128)} %param.8) | copy-start | bytes 2308
